TPU v7x, 32 devices: a whole 2x2x4 slice. The times are simulated.
32 devices in a mesh: dp: 8 (over z, x), tensor: 4 (over y, core).
Axes of the slice: x: 2, y: 2, z: 4, core: 2. Of those that a mesh axis runs over, the one named last changes fastest.
Arguments:
- block_input: bfloat16 [8192, 768], P('dp'), may hold values from -6 to 6
- block_order: int32 [1, 8], replicated, may hold values from 0 to 7, each once within a row
- attn_norm_gain: float32 [768], replicated, may hold values from 0.5 to 1.5
- attn_norm_bias: float32 [768], replicated, may hold values from -1.8 to 1.8
- input_weight: bfloat16 [3, 768, 768], P(None, None, 'tensor'), may hold values from -0.21875 to 0.21875
- query_value_bias: float32 [2, 768], P(None, 'tensor'), may hold values from -3 to 3
- output_weight: bfloat16 [768, 768], P('tensor'), may hold values from -3 to 3
- output_bias: float32 [768], replicated, may hold values from -1.8 to 1.8
- feed_norm_gain: float32 [768], replicated, may hold values from 0.5 to 1.5
- feed_norm_bias: float32 [768], replicated, may hold values from -1.8 to 1.8
- expand_weight: bfloat16 [768, 3072], P(None, 'tensor'), may hold values from -0.21875 to 0.21875
- expand_bias: float32 [3072], P('tensor'), may hold values from -3 to 3
- shrink_weight: bfloat16 [3072, 768], P('tensor'), may hold values from -0.109375 to 0.109375
- shrink_bias: float32 [768], replicated, may hold values from -1.8 to 1.8
- output_grad: bfloat16 [8192, 768], P('dp'), may hold values from -6 to 6
Outputs:
- block_output: bfloat16 [8192, 768], P('dp')
- input_grad: bfloat16 [8192, 768], P('dp')
- attn_norm_gain_grad: float32 [768], replicated
- attn_norm_bias_grad: float32 [768], replicated
- input_weight_grad: float32 [3, 768, 768], P(None, None, 'tensor')
- query_value_bias_grad: float32 [2, 768], P(None, 'tensor')
- output_weight_grad: float32 [768, 768], P('tensor')
- output_bias_grad: float32 [768], replicated
- feed_norm_gain_grad: float32 [768], replicated
- feed_norm_bias_grad: float32 [768], replicated
- expand_weight_grad: float32 [768, 3072], P(None, 'tensor')
- expand_bias_grad: float32 [3072], P('tensor')
- shrink_weight_grad: float32 [3072, 768], P('tensor')
- shrink_bias_grad: float32 [768], replicated
Inputs may be any that keep to these rules, and one draw needn't show every extreme that they name: Each row of block_order lists every block number 0 to 7 once.
All inputs are finite; a program needn't handle non-finite values.
Results may differ from a plain program's by a relative error of at most 0.018.
Values may be sent and summed in bfloat16 or wider, within the bound.
A program may use at most 128 MiB of HBM per device.

v0:
```python
import jax
import jax.numpy as jnp
from jax import lax
from jax.sharding import PartitionSpec as P

HEAD_DIM = 64
GROUP = 8


EPSILON = 1e-05
MASKED_SCORE = -1e30


def partner(value, axis, apart):
    mask = 2**apart
    pairs = [(source, source ^ mask) for source in range(lax.axis_size(axis))]
    return lax.ppermute(value, axis, pairs)


def layer_norm(rows, gain, bias_vec):
    center = jnp.mean(rows, axis=-1, keepdims=True)
    centred = rows - center
    spread = jnp.mean(centred * centred, axis=-1, keepdims=True)
    return centred * lax.rsqrt(spread + EPSILON) * gain + bias_vec


def gelu_tanh(values):
    return jax.nn.gelu(values, approximate=True)


def probs_of(scores, allowed, log_rows):
    return jnp.where(allowed, jnp.exp(scores - log_rows), 0.0)


def local(
    block_input,
    block_order,
    attn_norm_gain,
    attn_norm_bias,
    input_weight,
    query_value_bias,
    output_weight,
    output_bias,
    feed_norm_gain,
    feed_norm_bias,
    expand_weight,
    expand_bias,
    shrink_weight,
    shrink_bias,
    output_grad,
):
    dp_index = lax.axis_index("dp")
    tok_rows = block_input.shape[0]
    key_len = GROUP * tok_rows
    local_width = input_weight.shape[2]
    local_heads = local_width // HEAD_DIM
    scale = HEAD_DIM ** (-0.5)
    member = dp_index % GROUP
    seq_num = dp_index // GROUP
    order_row = lax.dynamic_index_in_dim(block_order, seq_num, 0, keepdims=False)
    own_block = lax.dynamic_index_in_dim(order_row, member, 0, keepdims=False)
    offsets = jnp.arange(tok_rows, dtype=jnp.int32)
    query_pos = own_block * tok_rows + offsets
    key_pos = (order_row[:, None] * tok_rows + offsets[None, :]).reshape(key_len)
    bit_count = GROUP.bit_length() - 1
    key_block_len = min(512, key_len)
    key_blocks = key_len // key_block_len
    key_pos_blocks = key_pos.reshape(key_blocks, key_block_len)

    def split_heads(rows):
        return rows.reshape(rows.shape[0], local_heads, HEAD_DIM)

    def is_upper(bit):
        return dp_index // 2**bit % 2 == 1

    def block_scores(query_rows, key_rows, query_places, key_places):
        scores = (
            jnp.einsum("qhd,khd->hqk", query_rows, key_rows, preferred_element_type=jnp.float32)
            * scale
        )
        allowed = key_places[None, None, :] <= query_places[None, :, None]
        return (scores, allowed)

    inputs32 = block_input.astype(jnp.float32)
    normed_one = layer_norm(inputs32, attn_norm_gain, attn_norm_bias).astype(jnp.bfloat16)
    projected = jnp.einsum(
        "td,jdf->jtf", normed_one, input_weight, preferred_element_type=jnp.float32
    )
    queries = (projected[0] + query_value_bias[0]).astype(jnp.bfloat16)
    keys_low = projected[1].astype(jnp.bfloat16)
    values_low = (projected[2] + query_value_bias[1]).astype(jnp.bfloat16)
    query_heads = split_heads(queries)
    key_value = jnp.concatenate([keys_low, values_low], axis=1)
    gathered = key_value
    for bit in range(bit_count):
        other = partner(gathered, "dp", bit)
        gathered = jnp.where(
            is_upper(bit),
            jnp.concatenate([other, gathered], axis=0),
            jnp.concatenate([gathered, other], axis=0),
        )
    kv_blocks = gathered.reshape(key_blocks, key_block_len, 2 * local_width)

    def norm_block(carried, inputs):
        run_max, run_sum = carried
        kv_rows, places = inputs
        scores, allowed = block_scores(
            query_heads, split_heads(kv_rows[:, :local_width]), query_pos, places
        )
        masked = jnp.where(allowed, scores, MASKED_SCORE)
        new_max = jnp.maximum(run_max, jnp.max(masked, axis=-1))
        fresh = jnp.where(allowed, jnp.exp(masked - new_max[:, :, None]), 0.0)
        run_sum = run_sum * jnp.exp(run_max - new_max) + jnp.sum(fresh, axis=-1)
        return ((new_max, run_sum), None)

    start_max = jnp.full((local_heads, tok_rows), MASKED_SCORE, jnp.float32)
    start_sum = jnp.zeros((local_heads, tok_rows), jnp.float32)
    (run_max, run_sum), unused_norm_ys = lax.scan(
        norm_block, (start_max, start_sum), (kv_blocks, key_pos_blocks)
    )
    log_total = run_max + jnp.log(run_sum)

    def context_block(carried, inputs):
        kv_rows, places = inputs
        scores, allowed = block_scores(
            query_heads, split_heads(kv_rows[:, :local_width]), query_pos, places
        )
        weights = probs_of(scores, allowed, log_total[:, :, None]).astype(jnp.bfloat16)
        return (
            carried
            + jnp.einsum(
                "hqk,khd->qhd",
                weights,
                split_heads(kv_rows[:, local_width:]),
                preferred_element_type=jnp.float32,
            ),
            None,
        )

    zero_heads = jnp.zeros((tok_rows, local_heads, HEAD_DIM), jnp.float32)
    context, unused_context_ys = lax.scan(context_block, zero_heads, (kv_blocks, key_pos_blocks))
    context_low = context.reshape(tok_rows, local_width).astype(jnp.bfloat16)
    attn_part = jnp.dot(context_low, output_weight, preferred_element_type=jnp.float32)
    resid = (
        inputs32
        + lax.psum(attn_part.astype(jnp.bfloat16), "tensor").astype(jnp.float32)
        + output_bias
    )
    normed_two = layer_norm(resid, feed_norm_gain, feed_norm_bias).astype(jnp.bfloat16)
    hidden_pre = (
        jnp.dot(normed_two, expand_weight, preferred_element_type=jnp.float32) + expand_bias
    )
    hidden_low = gelu_tanh(hidden_pre).astype(jnp.bfloat16)
    feed_part = jnp.dot(hidden_low, shrink_weight, preferred_element_type=jnp.float32)
    block_output = (
        resid + lax.psum(feed_part.astype(jnp.bfloat16), "tensor").astype(jnp.float32) + shrink_bias
    ).astype(jnp.bfloat16)
    grad_out32 = output_grad.astype(jnp.float32)
    shrink_weight_grad = jnp.einsum(
        "tf,td->fd", hidden_low, output_grad, preferred_element_type=jnp.float32
    )
    shrink_bias_grad = jnp.sum(grad_out32, axis=0)
    hidden_grad = jnp.einsum(
        "td,fd->tf", output_grad, shrink_weight, preferred_element_type=jnp.float32
    )
    unused_value, gelu_pull = jax.vjp(gelu_tanh, hidden_pre)
    pre_grad = gelu_pull(hidden_grad)[0].astype(jnp.bfloat16)
    expand_weight_grad = jnp.einsum(
        "td,tf->df", normed_two, pre_grad, preferred_element_type=jnp.float32
    )
    expand_bias_grad = jnp.sum(pre_grad.astype(jnp.float32), axis=0)
    two_part = jnp.einsum("tf,df->td", pre_grad, expand_weight, preferred_element_type=jnp.float32)
    normed_two_grad = lax.psum(two_part.astype(jnp.bfloat16), "tensor").astype(jnp.float32)
    unused_norm, norm_two_pull = jax.vjp(layer_norm, resid, feed_norm_gain, feed_norm_bias)
    resid_part, feed_norm_gain_grad, feed_norm_bias_grad = norm_two_pull(normed_two_grad)
    resid_grad = grad_out32 + resid_part
    branch_grad = resid_grad.astype(jnp.bfloat16)
    output_weight_grad = jnp.einsum(
        "tc,td->cd", context_low, branch_grad, preferred_element_type=jnp.float32
    )
    output_bias_grad = jnp.sum(branch_grad.astype(jnp.float32), axis=0)
    context_grad = jnp.einsum(
        "td,cd->tc", branch_grad, output_weight, preferred_element_type=jnp.float32
    ).astype(jnp.bfloat16)
    grad_heads = split_heads(context_grad)
    delta = jnp.transpose(jnp.sum(grad_heads.astype(jnp.float32) * context, axis=-1))

    def back_block(query_sum, inputs):
        kv_rows, places = inputs
        key_heads = split_heads(kv_rows[:, :local_width])
        value_heads = split_heads(kv_rows[:, local_width:])
        scores, allowed = block_scores(query_heads, key_heads, query_pos, places)
        probs = probs_of(scores, allowed, log_total[:, :, None])
        prob_grad = jnp.einsum(
            "qhd,khd->hqk", grad_heads, value_heads, preferred_element_type=jnp.float32
        )
        score_grad = (probs * (prob_grad - delta[:, :, None])).astype(jnp.bfloat16)
        query_sum = (
            query_sum
            + jnp.einsum("hqk,khd->qhd", score_grad, key_heads, preferred_element_type=jnp.float32)
            * scale
        )
        key_part = (
            jnp.einsum("hqk,qhd->khd", score_grad, query_heads, preferred_element_type=jnp.float32)
            * scale
        )
        value_part = jnp.einsum(
            "hqk,qhd->khd",
            probs.astype(jnp.bfloat16),
            grad_heads,
            preferred_element_type=jnp.float32,
        )
        joined = jnp.concatenate(
            [
                key_part.reshape(key_block_len, local_width),
                value_part.reshape(key_block_len, local_width),
            ],
            axis=1,
        )
        return (query_sum, joined)

    query_acc, kv_terms = lax.scan(back_block, zero_heads, (kv_blocks, key_pos_blocks))
    remaining = kv_terms.reshape(key_len, 2 * local_width)
    for bit in reversed(range(bit_count)):
        half = remaining.shape[0] // 2
        lower = remaining[:half]
        higher = remaining[half:]
        outgoing = jnp.where(is_upper(bit), lower, higher)
        kept = jnp.where(is_upper(bit), higher, lower)
        remaining = kept + partner(outgoing.astype(jnp.bfloat16), "dp", bit).astype(outgoing.dtype)
    query_grad = query_acc.reshape(tok_rows, local_width)
    key_grad = remaining[:, :local_width]
    value_grad = remaining[:, local_width:]
    grads_low = jnp.stack([query_grad, key_grad, value_grad]).astype(jnp.bfloat16)
    input_weight_grad = jnp.einsum(
        "td,jtf->jdf", normed_one, grads_low, preferred_element_type=jnp.float32
    )
    query_value_bias_grad = jnp.stack(
        [
            jnp.sum(grads_low[0].astype(jnp.float32), axis=0),
            jnp.sum(grads_low[2].astype(jnp.float32), axis=0),
        ]
    )
    one_part = jnp.einsum(
        "jtf,jdf->td", grads_low, input_weight, preferred_element_type=jnp.float32
    )
    normed_one_grad = lax.psum(one_part.astype(jnp.bfloat16), "tensor").astype(jnp.float32)
    unused_first, norm_one_pull = jax.vjp(layer_norm, inputs32, attn_norm_gain, attn_norm_bias)
    input_part, attn_norm_gain_grad, attn_norm_bias_grad = norm_one_pull(normed_one_grad)
    input_grad = (resid_grad + input_part).astype(jnp.bfloat16)
    summed = lax.psum(
        (
            attn_norm_gain_grad,
            attn_norm_bias_grad,
            input_weight_grad,
            query_value_bias_grad,
            output_weight_grad,
            output_bias_grad,
            feed_norm_gain_grad,
            feed_norm_bias_grad,
            expand_weight_grad,
            expand_bias_grad,
            shrink_weight_grad,
            shrink_bias_grad,
        ),
        "dp",
    )
    return (
        block_output,
        input_grad,
        summed[0],
        summed[1],
        summed[2],
        summed[3],
        summed[4],
        summed[5],
        summed[6],
        summed[7],
        summed[8],
        summed[9],
        summed[10],
        summed[11],
    )


def solution(mesh):
    placed = (
        P("dp", None),
        P(),
        P(),
        P(),
        P(None, None, "tensor"),
        P(None, "tensor"),
        P("tensor", None),
        P(),
        P(),
        P(),
        P(None, "tensor"),
        P("tensor"),
        P("tensor", None),
        P(),
        P("dp", None),
    )
    return jax.shard_map(
        local,
        mesh=mesh,
        in_specs=placed,
        out_specs=(
            P("dp", None),
            P("dp", None),
            P(),
            P(),
            P(None, None, "tensor"),
            P(None, "tensor"),
            P("tensor", None),
            P(),
            P(),
            P(),
            P(None, "tensor"),
            P("tensor"),
            P("tensor", None),
            P(),
        ),
        check_vma=False,
    )
```

profile of v0, /device:TPU:0, one launch (start us, length us, event | category | flops | bytes accessed | tf_op | source)
XLA Modules:
  0.0 1296.5 jit_solution(6809413519017981205)
XLA Ops:
  19.3 17.9 %collective-permute-done = bf16[1024,384]{0,1:T(8,128)(2,1)} collective-permute-done((bf16[1024,384]{0,1:T(8,128)(2,1)}, bf16[1024,384]{0,1:T(8,128)(2,1)}, u32[]{:S(2)}, u32[]{:S(2)}) %collective-permute-start) | collective-permute-done | bytes 786464 | tf_op jit(solution)/shard_map/ppermute | solution.py:17
  42.2 34.1 %collective-permute-done.1 = bf16[2048,384]{0,1:T(8,128)(2,1)} collective-permute-done((bf16[2048,384]{0,1:T(8,128)(2,1)}, bf16[2048,384]{0,1:T(8,128)(2,1)}, u32[]{:S(2)}, u32[]{:S(2)}) %collective-permute-start.1) | collective-permute-done | bytes 1572896 | tf_op jit(solution)/shard_map/ppermute | solution.py:17
  76.3 5.1 maximum_select_fusion.1
  90.2 128.1 %collective-permute-done.2 = bf16[4096,384]{0,1:T(8,128)(2,1)} collective-permute-done((bf16[4096,384]{0,1:T(8,128)(2,1)}, bf16[4096,384]{0,1:T(8,128)(2,1)}, u32[]{:S(2)}, u32[]{:S(2)}) %collective-permute-start.2) | collective-permute-done | bytes 3145760 | tf_op jit(solution)/shard_map/ppermute | solution.py:17
  218.3 6.8 maximum_select_fusion
  228.4 93.3 %while.37 = (s32[]{:T(128)}, f32[3,1024]{1,0:T(4,128)S(1)}, f32[3,1024]{1,0:T(4,128)S(1)}, s32[16,512]{1,0:T(8,128)}, bf16[16,512,384]{1,2,0:T(8,128)(2,1)}, /*i...) while((s32[]{:T(128)}, f32[3,1024]{1,0:T(4,128)S(1)}, ...), condition=%wide.region_5.6_spmd.clone, body=%wide.region_2.5_spmd.clone.sunk | while | flops 214450176 | bytes 16099452 | solution.py:118
  322.4 131.9 %while.38 = (s32[]{:T(128)}, f32[1024,3,64]{0,2,1:T(8,128)}, bf16[16,512,384]{1,2,0:T(8,128)(2,1)}, s32[16,512]{1,0:T(8,128)}, bf16[1024,3,64]{2,1,0:T(4,128)(2,...) while((s32[]{:T(128)}, f32[1024,3,64]{0,2,1:T(8,128)}, ...), condition=%wide.region_7.8_spmd.clone, body=%wide.region_6.7_spmd.clone.sunk | while | flops 409863168 | bytes 5007483 | solution.py:141
  334.0 4.7 fusion.154
  342.3 4.7 fusion.154
  350.5 4.7 fusion.154
  358.8 4.7 fusion.154
  367.1 4.7 fusion.154
  375.3 4.7 fusion.154
  383.6 4.7 fusion.154
  391.8 4.7 fusion.154
  400.1 4.7 fusion.154
  408.4 4.7 fusion.154
  424.9 4.7 fusion.154
  433.1 4.7 fusion.154
  449.7 4.7 fusion.154
  459.5 43.4 %all-reduce.8.cloned.1.call-done = bf16[1024,768]{1,0:T(8,128)(2,1)} async-done(((bf16[1024,768]{1,0:T(8,128)(2,1)}), bf16[1024,768]{1,0:T(8,128)(2,1)}) %all-reduce.8.cloned.1.call-update) | async-done | bytes 1572880 | tf_op jit(solution)/shard_map/psum | solution.py:146
  516.1 43.0 %all-reduce.10.cloned.1.call-done = bf16[1024,768]{1,0:T(8,128)(2,1)} async-done(((bf16[1024,768]{1,0:T(8,128)(2,1)}), bf16[1024,768]{1,0:T(8,128)(2,1)}) %all-reduce.10.cloned.1.call-update) | async-done | bytes 1572880 | tf_op jit(solution)/shard_map/psum | solution.py:173
  571.1 193.8 %while.39 = (s32[]{:T(128)}, f32[1024,3,64]{0,2,1:T(8,128)}, f32[16,512,384]{1,2,0:T(8,128)}, bf16[16,512,384]{1,2,0:T(8,128)(2,1)}, s32[16,512]{1,0:T(8,128)}, ...) while((s32[]{:T(128)}, f32[1024,3,64]{0,2,1:T(8,128)}, ...), condition=%wide.region_17.18_spmd.clone, body=%wide.region_16.17_spmd.clone.sunk | while | flops 1023771648 | bytes 43944168 | solution.py:222
  764.9 5.3 fusion.57
  782.7 127.8 %collective-permute-done.3 = bf16[4096,384]{0,1:T(8,128)(2,1)S(1)} collective-permute-done((bf16[4096,384]{0,1:T(8,128)(2,1)}, bf16[4096,384]{0,1:T(8,128)(2,1)S(1)}, u32[]{:S(2)}, u32[]{:S(2)}) %collective-permute-start.3) | collective-permute-done | bytes 3145760 | tf_op jit(solution)/shard_map/ppermute | solution.py:17
  912.7 34.8 %collective-permute-done.4 = bf16[2048,384]{0,1:T(8,128)(2,1)S(1)} collective-permute-done((bf16[2048,384]{0,1:T(8,128)(2,1)S(1)}, bf16[2048,384]{0,1:T(8,128)(2,1)S(1)}, u32[]{:S(2)}, u32[]{:S(2)}) %collective-permute-start.4) | collective-permute-done | bytes 1572896 | tf_op jit(solution)/shard_map/ppermute | solution.py:17
  953.4 12.9 collective-permute-done.5
  970.6 5.8 fusion.79
  985.2 56.0 %all-reduce.14.cloned.1.call-done = (bf16[1024,768]{1,0:T(8,128)(2,1)}, bf16[1024,768]{1,0:T(8,128)(2,1)}) async-done(((bf16[1024,768]{1,0:T(8,128)(2,1)}, bf16[1024,768]{1,0:T(8,128)(2,1)}), (bf16[1024,768]{1,0:T(8,128)(2,1)}, bf16[1024,768]{1,0:T(8,128)(2,1)})) %all-reduce.14.cloned.1.call-update) | async-done | bytes 3145744 | tf_op jit(solution)/shard_map/psum | solution.py:156
  1046.1 5.7 add_convert_fusion
  1051.8 40.0 %all-reduce = (f32[768]{0:T(1024)}, f32[768]{0:T(1024)}, f32[2,192]{1,0:T(2,128)}, f32[768]{0:T(1024)}, f32[768]{0:T(1024)}, /*index=5*/f32[768]{0:T(1024)}, f32[768]{0:T(1024)}, f32[768]{0:T(1024)}) all-reduce(f32[768]{0:T(1024)S(1)} %get-tuple-element.287, ...), channel_id=1, replica_groups=mesh['dp'=8,'tensor'=4] {'dp'}, use_global_device_ids=true, to_apply=%region_22.23 | all-reduce | flops 5760 | bytes 46080 | tf_op jit(solution)/shard_map/psum | solution.py:251
  1091.8 191.3 %all-reduce.12.cloned.1.call-done = (f32[3,768,192]{1,2,0:T(8,128)}, f32[192,768]{1,0:T(8,128)}, f32[768,768]{1,0:T(8,128)}, f32[768,768]{1,0:T(8,128)}) async-done(((f32[3,768,192]{1,2,0:T(8,128)}, f32[192,768]{1,0:T(8,128)}, f32[768,768]{1,0:T(8,128)}, f32[768,768]{1,0:T(8,128)}), (f32[3,768,192]{1,2,0:T(8,128)}, f32[192,768]{1,0:T(8,128)}, f32[768,768]{1,0:T(8,128)}, ...) | async-done | bytes 7077904 | tf_op jit(solution)/shard_map/psum | solution.py:251
  (736 shorter events, 459.9 us)
Async XLA Ops:
  7.2 500.7 %copy-start = (bf16[768,768]{1,0:T(8,128)(2,1)S(1)}, bf16[768,768]{1,0:T(8,128)(2,1)}, u32[]{:S(2)}) copy-start(bf16[768,768]{1,0:T(8,128)(2,1)} %param.33) | copy-start | bytes 3538948
  7.2 495.6 %all-reduce.8.cloned.1.call-start = ((), (), s32[]{:S(2)}) async-start(), calls=%async_computation | async-start | bytes 3145728 | tf_op jit(solution)/shard_map/psum | solution.py:146
  16.4 20.8 %collective-permute-start = (bf16[1024,384]{0,1:T(8,128)(2,1)}, bf16[1024,384]{0,1:T(8,128)(2,1)}, u32[]{:S(2)}, u32[]{:S(2)}) collective-permute-start(bf16[1024,384]{0,1:T(8,128)(2,1)} %pad_maximum_fusion.1), channel_id=1, source_target_pairs={{0,4},{4,0},{8,12},{12,8},{16,20},{20,16},{24,28},{28,24},{1,5},{5... | collective-permute-start | bytes 2359304 | tf_op jit(solution)/shard_map/ppermute | solution.py:17
  40.4 35.9 %collective-permute-start.1 = (bf16[2048,384]{0,1:T(8,128)(2,1)}, bf16[2048,384]{0,1:T(8,128)(2,1)}, u32[]{:S(2)}, u32[]{:S(2)}) collective-permute-start(bf16[2048,384]{0,1:T(8,128)(2,1)} %maximum_select_fusion.2), channel_id=1, source_target_pairs={{0,8},{4,12},{8,0},{12,4},{16,24},{20,28},{24,16},{28,20},{1,9},{5... | collective-permute-start | bytes 4718600 | tf_op jit(solution)/shard_map/ppermute | solution.py:17
  42.2 43.8 %copy-start.66 = (s32[1,8]{1,0:T(1,128)S(1)}, s32[1,8]{1,0:T(1,128)}, u32[]{:S(2)}) copy-start(s32[1,8]{1,0:T(1,128)} %param.22) | copy-start | bytes 100
  81.3 137.0 %collective-permute-start.2 = (bf16[4096,384]{0,1:T(8,128)(2,1)}, bf16[4096,384]{0,1:T(8,128)(2,1)}, u32[]{:S(2)}, u32[]{:S(2)}) collective-permute-start(bf16[4096,384]{0,1:T(8,128)(2,1)} %maximum_select_fusion.1), channel_id=1, source_target_pairs={{0,16},{4,20},{8,24},{12,28},{16,0},{20,4},{24,8},{28,12},{1,17},{... | collective-permute-start | bytes 9437192 | tf_op jit(solution)/shard_map/ppermute | solution.py:17
  454.3 48.5 %copy-start.32 = (f32[768]{0:T(1024)S(1)}, f32[768]{0:T(1024)}, u32[]{:S(2)}) copy-start(f32[768]{0:T(1024)} %param.28) | copy-start | bytes 9220
  459.0 46.8 %copy-start.38 = (f32[768]{0:T(1024)S(1)}, f32[768]{0:T(1024)}, u32[]{:S(2)}) copy-start(f32[768]{0:T(1024)} %param.29) | copy-start | bytes 9220
  459.1 46.8 %copy-start.62 = (f32[768]{0:T(1024)S(1)}, f32[768]{0:T(1024)}, u32[]{:S(2)}) copy-start(f32[768]{0:T(1024)} %param.30) | copy-start | bytes 9220
  459.1 100.0 %all-reduce.10.cloned.1.call-start = ((), (), s32[]{:S(2)}) async-start(), calls=%async_computation.1 | async-start | bytes 3145728 | tf_op jit(solution)/shard_map/psum | solution.py:173
  505.9 60.1 %copy-start.35 = (f32[1024]{0:T(1024)}, f32[1024]{0:T(1024)S(1)}, u32[]{:S(2)}) copy-start(f32[1024]{0:T(1024)S(1)} %fusion.71) | copy-start | bytes 12292
  516.0 525.2 %all-reduce.14.cloned.1.call-start = ((), (), s32[]{:S(2)}) async-start(), calls=%async_computation.3 | async-start | bytes 6291456 | tf_op jit(solution)/shard_map/psum | solution.py:156
  764.9 9.8 copy-start.9
  772.3 138.2 %collective-permute-start.3 = (bf16[4096,384]{0,1:T(8,128)(2,1)}, bf16[4096,384]{0,1:T(8,128)(2,1)S(1)}, u32[]{:S(2)}, u32[]{:S(2)}) collective-permute-start(bf16[4096,384]{0,1:T(8,128)(2,1)} %bitcast.52), channel_id=1, source_target_pairs={{0,16},{4,20},{8,24},{12,28},{16,0},{20,4},{24,8},{28,12},{1,17},{... | collective-permute-start | bytes 9437192 | tf_op jit(solution)/shard_map/ppermute | solution.py:17
  912.0 38.0 %copy-start.61 = (f32[768]{0:T(1024)S(1)}, f32[768]{0:T(1024)}, u32[]{:S(2)}) copy-start(f32[768]{0:T(1024)} %param.32) | copy-start | bytes 9220
  912.1 38.0 %copy-start.68 = (f32[1024,768]{1,0:T(8,128)S(1)}, f32[1024,768]{1,0:T(8,128)}, u32[]{:S(2)}) copy-start(f32[1024,768]{1,0:T(8,128)} %copy-done.67) | copy-start | bytes 9437188
  912.1 35.4 %collective-permute-start.4 = (bf16[2048,384]{0,1:T(8,128)(2,1)S(1)}, bf16[2048,384]{0,1:T(8,128)(2,1)S(1)}, u32[]{:S(2)}, u32[]{:S(2)}) collective-permute-start(bf16[2048,384]{0,1:T(8,128)(2,1)S(1)} %select_convert_fusion.1), channel_id=1, source_target_pairs={{0,8},{4,12},{8,0},{12,4},{16,24},{20,28},{24,16},{28,20},{1,9},{5... | collective-permute-start | bytes 4718600 | tf_op jit(solution)/shard_map/ppermute | solution.py:17
  948.5 17.8 %collective-permute-start.5 = (bf16[1024,384]{0,1:T(8,128)(2,1)S(1)}, bf16[1024,384]{0,1:T(8,128)(2,1)S(1)}, u32[]{:S(2)}, u32[]{:S(2)}) collective-permute-start(bf16[1024,384]{0,1:T(8,128)(2,1)S(1)} %select_convert_fusion.2), channel_id=1, source_target_pairs={{0,4},{4,0},{8,12},{12,8},{16,20},{20,16},{24,28},{28,24},{1,5},{5... | collective-permute-start | bytes 2359304 | tf_op jit(solution)/shard_map/ppermute | solution.py:17
  953.3 13.5 %copy-start.24 = (bf16[1024,3,64]{0,2,1:T(8,128)(2,1)}, bf16[1024,3,64]{0,2,1:T(8,128)(2,1)S(1)}, u32[]{:S(2)}) copy-start(bf16[1024,3,64]{0,2,1:T(8,128)(2,1)S(1)} %convert.16) | copy-start | bytes 1179652
  953.3 14.3 %copy-start.59 = (bf16[3,768,192]{1,2,0:T(8,128)(2,1)S(1)}, bf16[3,768,192]{1,2,0:T(8,128)(2,1)}, u32[]{:S(2)}) copy-start(bf16[3,768,192]{1,2,0:T(8,128)(2,1)} %param.25) | copy-start | bytes 2654212
  970.3 312.9 %all-reduce.12.cloned.1.call-start = ((), (), s32[]{:S(2)}) async-start(), calls=%async_computation.2 | async-start | bytes 14155776 | tf_op jit(solution)/shard_map/psum | solution.py:251
  970.5 5.9 copy-start.4
  970.5 5.9 copy-start.36
  970.6 5.9 copy-start.39
  970.6 5.9 copy-start.63
  970.6 5.9 copy-start.70
  985.1 58.8 %copy-start.50 = (f32[1024]{0:T(1024)S(1)}, f32[1024]{0:T(1024)}, u32[]{:S(2)}) copy-start(f32[1024]{0:T(1024)} %copy-done.49) | copy-start | bytes 12292
  985.2 58.8 %copy-start.43 = (f32[768]{0:T(1024)S(1)}, f32[768]{0:T(1024)}, u32[]{:S(2)}) copy-start(f32[768]{0:T(1024)} %param.23) | copy-start | bytes 9220
  985.2 58.8 %copy-start.46 = (f32[1024]{0:T(1024)S(1)}, f32[1024]{0:T(1024)}, u32[]{:S(2)}) copy-start(f32[1024]{0:T(1024)} %copy-done.44) | copy-start | bytes 12292
  1046.0 5.8 copy-start.52
  1046.0 5.8 copy-start.53
  1046.1 5.8 copy-start.54
  (94 other events, 236.1 us)
Sparse Core Ops, SparseCore 0:
  459.2 43.6 all-reduce.7
  516.1 42.8 all-reduce.9
  970.4 70.8 all-reduce.13
  1046.7 236.4 all-reduce.11
where the time goes:
time: 1310 us; the launch traced here: 1300 us
  waiting for transfers between devices  689 us (53%)
  matrix products  258 us (20%)
  other arithmetic  164 us (13%)
  local copies, waits for them, and re-layouts  114 us (9%)
  blocking collectives  40 us (3%)
  between operations  14.9 us (1%)
    ppermute x6, waiting for transfers between devices, partner(): return lax.ppermute(value, axis, pairs)  356 us
    psum x1, waiting for transfers between devices, local(): lax.psum((attn_norm_gain_grad, attn_norm_bias_grad, input_weight_grad, qu...  191 us
    dot_general x16, matrix products, context_block(): jnp.einsum('hqk,khd->qhd', weights, split_heads(kv_rows[:, local_width:])...  74.5 us
    psum x1, waiting for transfers between devices, local(): lax.psum(feed_part.astype(jnp.bfloat16), 'tensor').astype(jnp.float32)  56 us
    squeeze x48, local copies, waits for them, and re-layouts, local(): lax.scan(norm_block, (start_max, start_sum), (kv_blocks, key_pos_blocks))  49.4 us
    dot_general x16, matrix products, back_block(): jnp.einsum('qhd,khd->hqk', grad_heads, value_heads, preferred_element_typ...  47.7 us
    psum x1, waiting for transfers between devices, local(): lax.psum(attn_part.astype(jnp.bfloat16), 'tensor').astype(jnp.float32)  43.4 us
    psum x1, waiting for transfers between devices, local(): lax.psum(two_part.astype(jnp.bfloat16), 'tensor').astype(jnp.float32)  43 us
  transfers between devices with their start and end apart: 10, of which 10 were waited for; matrix products, arithmetic and copies ran while one was open for 3% of the time, Pallas kernels for 0%

commit v1 on v0

v1 whole, which is shorter than its diff:
```python
import functools

import jax
import jax.numpy as jnp
from jax import lax
from jax.experimental import pallas as pl
from jax.experimental.pallas import tpu as pltpu
from jax.sharding import PartitionSpec as P

HEAD_DIM = 64
GROUP = 8


EPSILON = 1e-05
MASKED_SCORE = -1e30
RING = (0, 2, 4, 6, 7, 5, 3, 1)
TILE = 256
VMEM_BYTES = 48 * 1024 * 1024


def ring_shift(value, step):
    pairs = []
    for first in range(0, lax.axis_size("dp"), GROUP):
        for place in range(GROUP):
            pairs.append((first + RING[place], first + RING[(place + step) % GROUP]))
    return lax.ppermute(value, "dp", pairs)


def tdot(left, right, left_dim, right_dim):
    return lax.dot_general(
        left, right, (((left_dim,), (right_dim,)), ((), ())), preferred_element_type=jnp.float32
    )


def forward_kernel(heads, blocks, diagonal, *refs):
    flags, q_ref = refs[:2]
    kv_refs = refs[2 : 2 + 2 * blocks]
    carry_in = refs[2 + 2 * blocks : -3]
    max_ref, sum_ref, acc_ref = refs[-3:]
    tile = q_ref.shape[1]
    if diagonal:
        max_ref[...] = jnp.full(max_ref.shape, MASKED_SCORE, jnp.float32)
        sum_ref[...] = jnp.zeros(sum_ref.shape, jnp.float32)
        acc_ref[...] = jnp.zeros(acc_ref.shape, jnp.float32)
    else:
        max_ref[...] = carry_in[0][...]
        sum_ref[...] = carry_in[1][...]
        acc_ref[...] = carry_in[2][...]
    first_query = pl.program_id(0) * tile

    def block(k_ref, v_ref):
        for head in range(heads):
            rows = slice(head * HEAD_DIM, (head + 1) * HEAD_DIM)
            scores = tdot(k_ref[rows, :], q_ref[rows, :], 0, 0)
            if diagonal:
                key_place = lax.broadcasted_iota(jnp.int32, scores.shape, 0)
                query_place = lax.broadcasted_iota(jnp.int32, scores.shape, 1) + first_query
                scores = jnp.where(key_place <= query_place, scores, MASKED_SCORE)
            old = max_ref[head : head + 1, :]
            new = jnp.maximum(old, jnp.max(scores, axis=0, keepdims=True))
            weights = jnp.exp(scores - new)
            shrink = jnp.exp(old - new)
            max_ref[head : head + 1, :] = new
            sum_ref[head : head + 1, :] = sum_ref[head : head + 1, :] * shrink + jnp.sum(
                weights, axis=0, keepdims=True
            )
            acc_ref[rows, :] = acc_ref[rows, :] * shrink + tdot(
                v_ref[rows, :], weights.astype(jnp.bfloat16), 1, 0
            )

    for index in range(blocks):
        k_ref, v_ref = kv_refs[2 * index : 2 * index + 2]
        if diagonal:
            block(k_ref, v_ref)
        else:
            pl.when(flags[index] > 0)(functools.partial(block, k_ref, v_ref))


def attend_forward(flags, query_t, blocks, carried):
    width, tokens = query_t.shape
    heads = width // HEAD_DIM
    diagonal = carried is None
    in_specs = [
        pl.BlockSpec(memory_space=pltpu.SMEM),
        pl.BlockSpec((width, TILE), lambda i: (0, i)),
    ]
    operands = [flags, query_t]
    for pair in blocks:
        for array, half in pair:
            in_specs.append(pl.BlockSpec((width, tokens), lambda i, half=half: (half, 0)))
            operands.append(array)
    carry_specs = [
        pl.BlockSpec((heads, TILE), lambda i: (0, i)),
        pl.BlockSpec((heads, TILE), lambda i: (0, i)),
        pl.BlockSpec((width, TILE), lambda i: (0, i)),
    ]
    if not diagonal:
        in_specs.extend(carry_specs)
        operands.extend(carried)
    pairs = len(blocks) * heads * tokens * tokens
    return pl.pallas_call(
        functools.partial(forward_kernel, heads, len(blocks), diagonal),
        grid=(tokens // TILE,),
        in_specs=in_specs,
        out_specs=carry_specs,
        out_shape=[
            jax.ShapeDtypeStruct((heads, tokens), jnp.float32),
            jax.ShapeDtypeStruct((heads, tokens), jnp.float32),
            jax.ShapeDtypeStruct((width, tokens), jnp.float32),
        ],
        compiler_params=pltpu.CompilerParams(vmem_limit_bytes=VMEM_BYTES),
        cost_estimate=pl.CostEstimate(
            flops=16 * pairs * HEAD_DIM, bytes_accessed=4 * width * tokens * 4, transcendentals=pairs
        ),
    )(*operands)


def backward_kernel(heads, blocks, diagonal, *refs):
    flags, q_ref, grad_ref, log_ref, delta_ref = refs[:5]
    kv_refs = refs[5 : 5 + 2 * blocks]
    query_in = refs[5 + 2 * blocks]
    query_out = refs[6 + 2 * blocks]
    kv_out = refs[7 + 2 * blocks :]
    step = pl.program_id(0)
    tile = kv_refs[0].shape[1]
    width = heads * HEAD_DIM

    @pl.when(step == 0)
    def start():
        query_out[...] = query_in[...]

    def block(k_ref, v_ref, out_ref):
        for head in range(heads):
            rows = slice(head * HEAD_DIM, (head + 1) * HEAD_DIM)
            query = q_ref[rows, :]
            grad = grad_ref[rows, :]
            key = k_ref[rows, :]
            scores = tdot(key, query, 0, 0)
            probs = jnp.exp(scores - log_ref[head : head + 1, :])
            if diagonal:
                key_place = lax.broadcasted_iota(jnp.int32, scores.shape, 0) + step * tile
                query_place = lax.broadcasted_iota(jnp.int32, scores.shape, 1)
                probs = jnp.where(key_place <= query_place, probs, 0.0)
            prob_grad = tdot(v_ref[rows, :], grad, 0, 0)
            score_grad = (probs * (prob_grad - delta_ref[head : head + 1, :])).astype(jnp.bfloat16)
            out_ref[:, rows] = tdot(score_grad, query, 1, 1)
            out_ref[:, width + head * HEAD_DIM : width + (head + 1) * HEAD_DIM] = tdot(
                probs.astype(jnp.bfloat16), grad, 1, 1
            )
            query_out[rows, :] += tdot(key, score_grad, 1, 0)

    for index in range(blocks):
        k_ref, v_ref = kv_refs[2 * index : 2 * index + 2]
        out_ref = kv_out[index]
        if diagonal:
            block(k_ref, v_ref, out_ref)
        else:
            pl.when(flags[index] > 0)(functools.partial(block, k_ref, v_ref, out_ref))

            @pl.when(flags[index] <= 0)
            def empty(out_ref=out_ref):
                out_ref[...] = jnp.zeros(out_ref.shape, jnp.float32)


def attend_backward(flags, query_t, grad_t, log_total, delta, blocks, query_sum, diagonal):
    width, tokens = query_t.shape
    heads = width // HEAD_DIM
    whole = lambda rows: pl.BlockSpec((rows, tokens), lambda i: (0, 0))
    in_specs = [
        pl.BlockSpec(memory_space=pltpu.SMEM),
        whole(width),
        whole(width),
        whole(heads),
        whole(heads),
    ]
    operands = [flags, query_t, grad_t, log_total, delta]
    for pair in blocks:
        for array, half in pair:
            in_specs.append(pl.BlockSpec((width, TILE), lambda i, half=half: (half, i)))
            operands.append(array)
    in_specs.append(whole(width))
    operands.append(query_sum)
    pairs = len(blocks) * heads * tokens * tokens
    return pl.pallas_call(
        functools.partial(backward_kernel, heads, len(blocks), diagonal),
        grid=(tokens // TILE,),
        in_specs=in_specs,
        out_specs=[whole(width)]
        + [pl.BlockSpec((TILE, 2 * width), lambda i: (i, 0)) for unused in blocks],
        out_shape=[jax.ShapeDtypeStruct((width, tokens), jnp.float32)]
        + [jax.ShapeDtypeStruct((tokens, 2 * width), jnp.float32) for unused in blocks],
        compiler_params=pltpu.CompilerParams(vmem_limit_bytes=VMEM_BYTES),
        cost_estimate=pl.CostEstimate(
            flops=40 * pairs * HEAD_DIM, bytes_accessed=6 * width * tokens * 4, transcendentals=pairs
        ),
    )(*operands)


def layer_norm(rows, gain, bias_vec):
    center = jnp.mean(rows, axis=-1, keepdims=True)
    centred = rows - center
    spread = jnp.mean(centred * centred, axis=-1, keepdims=True)
    return centred * lax.rsqrt(spread + EPSILON) * gain + bias_vec


def gelu_tanh(values):
    return jax.nn.gelu(values, approximate=True)


def sum_tokens(value):
    return lax.psum(value, "dp")


def sum_tensor(value):
    return lax.psum(value.astype(jnp.bfloat16), "tensor").astype(jnp.float32)


def local(
    block_input,
    block_order,
    attn_norm_gain,
    attn_norm_bias,
    input_weight,
    query_value_bias,
    output_weight,
    output_bias,
    feed_norm_gain,
    feed_norm_bias,
    expand_weight,
    expand_bias,
    shrink_weight,
    shrink_bias,
    output_grad,
):
    dp_index = lax.axis_index("dp")
    tok_rows = block_input.shape[0]
    local_width = input_weight.shape[2]
    local_heads = local_width // HEAD_DIM
    scale = HEAD_DIM ** (-0.5)
    order_row = lax.dynamic_index_in_dim(block_order, dp_index // GROUP, 0, keepdims=False)
    ring_order = order_row[jnp.array(RING)]
    ring_place = jnp.argmax(jnp.array(RING) == dp_index % GROUP).astype(jnp.int32)
    own_block = ring_order[ring_place]

    def flags_of(*offsets):
        return jnp.stack(
            [
                (ring_order[(ring_place + offset) % GROUP] < own_block).astype(jnp.int32)
                for offset in offsets
            ]
        )

    inputs32 = block_input.astype(jnp.float32)
    normed_one = layer_norm(inputs32, attn_norm_gain, attn_norm_bias).astype(jnp.bfloat16)
    kv_weight = jnp.concatenate([input_weight[1], input_weight[2]], axis=1)
    kv_bias = jnp.concatenate([jnp.zeros((local_width,), jnp.float32), query_value_bias[1]])
    kv_t = (
        jnp.einsum("td,df->ft", normed_one, kv_weight, preferred_element_type=jnp.float32)
        + kv_bias[:, None]
    ).astype(jnp.bfloat16)
    ups = [kv_t]
    downs = [kv_t]
    ups.append(ring_shift(ups[0], 1))
    downs.append(ring_shift(downs[0], -1))
    query_t = (
        jnp.einsum("td,df->ft", normed_one, input_weight[0], preferred_element_type=jnp.float32)
        + query_value_bias[0][:, None]
    ).astype(jnp.bfloat16)
    query_t = query_t * jnp.bfloat16(scale)
    for hop in (2, 3):
        ups.append(ring_shift(ups[-1], 1))
        downs.append(ring_shift(downs[-1], -1))
    far_keys = ring_shift(ups[-1][:local_width], 1)
    far_values = ring_shift(downs[-1][local_width:], -1)

    def whole_pair(array):
        return ((array, 0), (array, 1))

    own_pair = [whole_pair(kv_t)]
    hop_pairs = [None] + [[whole_pair(ups[hop]), whole_pair(downs[hop])] for hop in (1, 2, 3)]
    far_pair = [((far_keys, 0), (far_values, 0))]
    hop_flags = [None] + [flags_of(-hop, hop) for hop in (1, 2, 3)]
    far_flags = flags_of(4)

    carried = attend_forward(far_flags, query_t, own_pair, None)
    for hop in (1, 2, 3):
        carried = attend_forward(hop_flags[hop], query_t, hop_pairs[hop], carried)
    run_max, run_sum, acc = attend_forward(far_flags, query_t, far_pair, carried)
    log_total = run_max + jnp.log(run_sum)
    context_t = (acc.reshape(local_heads, HEAD_DIM, tok_rows) / run_sum[:, None, :]).reshape(
        local_width, tok_rows
    )
    context_low_t = context_t.astype(jnp.bfloat16)
    attn_part = jnp.einsum(
        "ct,cd->td", context_low_t, output_weight, preferred_element_type=jnp.float32
    )
    resid = inputs32 + sum_tensor(attn_part) + output_bias
    normed_two = layer_norm(resid, feed_norm_gain, feed_norm_bias).astype(jnp.bfloat16)
    hidden_pre = (
        jnp.dot(normed_two, expand_weight, preferred_element_type=jnp.float32) + expand_bias
    )
    hidden_grad = jnp.einsum(
        "td,fd->tf", output_grad, shrink_weight, preferred_element_type=jnp.float32
    )
    hidden, gelu_pull = jax.vjp(gelu_tanh, hidden_pre)
    hidden_low = hidden.astype(jnp.bfloat16)
    pre_grad = gelu_pull(hidden_grad)[0].astype(jnp.bfloat16)
    two_part = jnp.einsum("tf,df->td", pre_grad, expand_weight, preferred_element_type=jnp.float32)
    normed_two_grad = sum_tensor(two_part)
    feed_part = jnp.dot(hidden_low, shrink_weight, preferred_element_type=jnp.float32)
    block_output = (resid + sum_tensor(feed_part) + shrink_bias).astype(jnp.bfloat16)
    grad_out32 = output_grad.astype(jnp.float32)
    shrink_weight_grad = jnp.einsum(
        "tf,td->fd", hidden_low, output_grad, preferred_element_type=jnp.float32
    )
    expand_weight_grad = jnp.einsum(
        "td,tf->df", normed_two, pre_grad, preferred_element_type=jnp.float32
    )
    feed_grads = sum_tokens(
        jnp.concatenate([shrink_weight_grad, expand_weight_grad], axis=0).astype(jnp.bfloat16)
    ).astype(jnp.float32)
    shrink_bias_grad = jnp.sum(grad_out32, axis=0)
    expand_bias_grad = jnp.sum(pre_grad.astype(jnp.float32), axis=0)
    unused_norm, norm_two_pull = jax.vjp(layer_norm, resid, feed_norm_gain, feed_norm_bias)
    resid_part, feed_norm_gain_grad, feed_norm_bias_grad = norm_two_pull(normed_two_grad)
    resid_grad = grad_out32 + resid_part
    branch_grad = resid_grad.astype(jnp.bfloat16)
    output_bias_grad = jnp.sum(branch_grad.astype(jnp.float32), axis=0)
    grad_t = jnp.einsum(
        "td,cd->ct", branch_grad, output_weight, preferred_element_type=jnp.float32
    ).astype(jnp.bfloat16)
    delta = jnp.sum(
        (grad_t.astype(jnp.float32) * context_t).reshape(local_heads, HEAD_DIM, tok_rows), axis=1
    )

    def back(flags, blocks, query_sum, diagonal):
        return attend_backward(
            flags, query_t, grad_t, log_total, delta, blocks, query_sum, diagonal
        )

    query_sum = jnp.zeros((local_width, tok_rows), jnp.float32)
    query_sum, far_term = back(far_flags, far_pair, query_sum, False)
    far_low = far_term.astype(jnp.bfloat16)
    moving_up = ring_shift(far_low[:, :local_width], 1)
    moving_down = ring_shift(far_low[:, local_width:], -1)
    for hop in (3, 2, 1):
        query_sum, down_term, up_term = back(hop_flags[hop], hop_pairs[hop], query_sum, False)
        if hop == 3:
            up_sum = jnp.concatenate(
                [
                    up_term[:, :local_width] + moving_up.astype(jnp.float32),
                    up_term[:, local_width:],
                ],
                axis=1,
            )
            down_sum = jnp.concatenate(
                [
                    down_term[:, :local_width],
                    down_term[:, local_width:] + moving_down.astype(jnp.float32),
                ],
                axis=1,
            )
        else:
            up_sum = up_term + moving_up.astype(jnp.float32)
            down_sum = down_term + moving_down.astype(jnp.float32)
        moving_up = ring_shift(up_sum.astype(jnp.bfloat16), 1)
        moving_down = ring_shift(down_sum.astype(jnp.bfloat16), -1)
    query_sum, own_term = back(far_flags, own_pair, query_sum, True)
    kv_low = (
        own_term + moving_up.astype(jnp.float32) + moving_down.astype(jnp.float32)
    ).astype(jnp.bfloat16)
    query_low_t = (query_sum * scale).astype(jnp.bfloat16)
    one_part = jnp.einsum(
        "ft,df->td", query_low_t, input_weight[0], preferred_element_type=jnp.float32
    ) + jnp.einsum("tf,df->td", kv_low, kv_weight, preferred_element_type=jnp.float32)
    normed_one_grad = sum_tensor(one_part)
    output_weight_grad_t = jnp.einsum(
        "ct,td->dc", context_low_t, branch_grad, preferred_element_type=jnp.float32
    )
    query_weight_grad = jnp.einsum(
        "td,ft->df", normed_one, query_low_t, preferred_element_type=jnp.float32
    )
    kv_weight_grad = jnp.einsum(
        "td,tf->df", normed_one, kv_low, preferred_element_type=jnp.float32
    )
    attn_grads = sum_tokens(
        jnp.concatenate(
            [query_weight_grad, kv_weight_grad, output_weight_grad_t], axis=1
        ).astype(jnp.bfloat16)
    ).astype(jnp.float32)
    input_weight_grad = jnp.stack(
        [attn_grads[:, j * local_width : (j + 1) * local_width] for j in range(3)]
    )
    output_weight_grad = jnp.transpose(attn_grads[:, 3 * local_width :])
    query_bias_grad = jnp.sum(query_low_t.astype(jnp.float32), axis=1)
    value_bias_grad = jnp.sum(kv_low[:, local_width:].astype(jnp.float32), axis=0)
    unused_first, norm_one_pull = jax.vjp(layer_norm, inputs32, attn_norm_gain, attn_norm_bias)
    input_part, attn_norm_gain_grad, attn_norm_bias_grad = norm_one_pull(normed_one_grad)
    input_grad = (resid_grad + input_part).astype(jnp.bfloat16)
    vectors = [
        attn_norm_gain_grad,
        attn_norm_bias_grad,
        output_bias_grad,
        feed_norm_gain_grad,
        feed_norm_bias_grad,
        expand_bias_grad,
        shrink_bias_grad,
        query_bias_grad,
        value_bias_grad,
    ]
    joined = sum_tokens(jnp.concatenate(vectors))
    summed = []
    first = 0
    for vector in vectors:
        summed.append(joined[first : first + vector.shape[0]])
        first += vector.shape[0]
    ff_rows = shrink_weight.shape[0]
    return (
        block_output,
        input_grad,
        summed[0],
        summed[1],
        input_weight_grad,
        jnp.stack([summed[7], summed[8]]),
        output_weight_grad,
        summed[2],
        summed[3],
        summed[4],
        feed_grads[ff_rows:],
        summed[5],
        feed_grads[:ff_rows],
        summed[6],
    )


def solution(mesh):
    placed = (
        P("dp", None),
        P(),
        P(),
        P(),
        P(None, None, "tensor"),
        P(None, "tensor"),
        P("tensor", None),
        P(),
        P(),
        P(),
        P(None, "tensor"),
        P("tensor"),
        P("tensor", None),
        P(),
        P("dp", None),
    )
    return jax.shard_map(
        local,
        mesh=mesh,
        in_specs=placed,
        out_specs=(
            P("dp", None),
            P("dp", None),
            P(),
            P(),
            P(None, None, "tensor"),
            P(None, "tensor"),
            P("tensor", None),
            P(),
            P(),
            P(),
            P(None, "tensor"),
            P("tensor"),
            P("tensor", None),
            P(),
        ),
        check_vma=False,
    )
```

time: 1310 us -> 568 us (0.43)
  waiting for transfers between devices: 689 us -> 252 us
  matrix products: 258 us -> 32.8 us
  other arithmetic: 164 us -> 43 us
  Pallas kernels: 0 us -> 109 us
  local copies, waits for them, and re-layouts: 114 us -> 18.7 us
  starting transfers between devices: 12.6 us -> 37.3 us
  between operations: 14.9 us -> 31.1 us
    ppermute x6 -> x16, waiting for transfers between devices: 356 us -> 24.9 us  [ring_shift(): return lax.ppermute(value, 'dp', pairs)]
    dot_general x117 -> x9, matrix products: 235 us -> 11.8 us  [the longest x1 2.12 us: local(): jnp.einsum('tf,df->td', kv_low, kv_weight, preferred_element_type=jnp.flo...]
    pallas_call x0 -> x10, Pallas kernels: none -> 109 us  [the longest x5 55.8 us: attend_backward(): pl.pallas_call(functools.partial(backward_kernel, heads, len(blocks), dia...]
    psum x4, waiting for transfers between devices: 334 us -> 227 us  [the longest x3 134 us: sum_tensor(): return lax.psum(value.astype(jnp.bfloat16), 'tensor').astype(jnp.float32)]
    squeeze x48 -> x1, local copies, waits for them, and re-layouts: 49.4 us -> 0.04 us  [local(): kv_weight = jnp.concatenate([input_weight[1], input_weight[2]], axis=1)]
    dynamic_slice x48 -> x1, local copies, waits for them, and re-layouts: 34.7 us -> 0.63 us  [flags_of(): ring_order[(ring_place + offset) % GROUP] < own_block]
    add x68 -> x0, other arithmetic: 33.7 us -> none  [the longest x48 30.4 us: local(): query_pos = own_block * tok_rows + offsets]
    le x48 -> x0, other arithmetic: 30 us -> none  [block_scores(): allowed = key_places[None, None, :] <= query_places[None, :, None]]
  transfers between devices with their start and end apart: 10 -> 20, of which waited for: 10 -> 9; matrix products, arithmetic and copies ran while one was open for 3% -> 8% of each run, Pallas kernels for 0% -> 16%
where the time goes in v1:
time: 568 us; the launch traced here: 563 us
  waiting for transfers between devices  252 us (44%)
  Pallas kernels  109 us (19%)
  other arithmetic  43 us (8%)
  blocking collectives  39.5 us (7%)
  starting transfers between devices  37.3 us (7%)
  matrix products  32.8 us (6%)
  between operations  31.1 us (5%)
  local copies, waits for them, and re-layouts  18.7 us (3%)
    psum x3, waiting for transfers between devices, sum_tensor(): return lax.psum(value.astype(jnp.bfloat16), 'tensor').astype(jnp.float32)  134 us
    psum x1, waiting for transfers between devices, sum_tokens(): return lax.psum(value, 'dp')  93.1 us
    pallas_call x5, Pallas kernels, attend_backward(): pl.pallas_call(functools.partial(backward_kernel, heads, len(blocks), dia...  55.8 us
    pallas_call x5, Pallas kernels, attend_forward(): pl.pallas_call(functools.partial(forward_kernel, heads, len(blocks), diag...  53.1 us
    psum x1, blocking collectives, sum_tokens(): return lax.psum(value, 'dp')  39.5 us
    ppermute x16, starting transfers between devices, ring_shift(): return lax.ppermute(value, 'dp', pairs)  36.4 us
    ppermute x16, waiting for transfers between devices, ring_shift(): return lax.ppermute(value, 'dp', pairs)  24.9 us
    reduce_sum x4, other arithmetic, layer_norm(): return centred * lax.rsqrt(spread + EPSILON) * gain + bias_vec  12 us
  transfers between devices with their start and end apart: 20, of which 9 were waited for; matrix products, arithmetic and copies ran while one was open for 8% of the time, Pallas kernels for 16%

profile of v1, /device:TPU:0, one launch (start us, length us, event | category | flops | bytes accessed | tf_op | source)
XLA Modules:
  0.0 563.0 jit_solution(3340077325955339804)
XLA Ops:
  14.5 2.9 collective-permute-start.4
  39.6 8.5 %shard_map.272 = (f32[3,1024]{1,0:T(4,128)S(1)}, f32[3,1024]{1,0:T(4,128)S(1)}, f32[192,1024]{1,0:T(8,128)S(1)}) custom-call(s32[1]{0:T(128)S(6)} %convert_element_type.153.refs_0_, bf16[192,1024]{1,0:T(8,128)(2,1)S(1)} %fusion.30.refs_1_, bf16[384,1024]{1,0:T(8,128)(2,1)S(1)} %add_convert_fusion.9.refs_2_.refs_3_.refs_5_.refs_6_, ...), custom_call_target="tpu_custom_call" | custom-call | flops 3221225472 | bytes 3145728 | tf_op jit(solution)/shard_map/pallas_call | solution.py:101
  48.2 6.0 %collective-permute-done.5.refs_4_.refs_5_.refs_7_.refs_8_ = bf16[384,1024]{1,0:T(8,128)(2,1)S(1)} collective-permute-done((bf16[384,1024]{1,0:T(8,128)(2,1)S(1)}, bf16[384,1024]{1,0:T(8,128)(2,1)S(1)}, u32[]{:S(2)}, u32[]{:S(2)}) %collective-permute-start.5) | collective-permute-done | bytes 786464 | tf_op jit(solution)/shard_map/ppermute | solution.py:26
  57.6 9.2 %shard_map.273 = (f32[3,1024]{1,0:T(4,128)S(1)}, f32[3,1024]{1,0:T(4,128)S(1)}, f32[192,1024]{1,0:T(8,128)S(1)}) custom-call(s32[2]{0:T(128)S(1)} %add_convert_fusion.14.refs_0_, bf16[192,1024]{1,0:T(8,128)(2,1)S(1)} %fusion.30.refs_1_, bf16[384,1024]{1,0:T(8,128)(2,1)S(1)} %copy-done.10, bf16[384,1024]{1,0:T(8,128)(2,1)S(1)} %copy-done.10, ...), custom_call_target="tpu_custom_call" | custom-call | flops 6442450944 | bytes 3145728 | tf_op jit(solution)/shard_map/pallas_call | solution.py:101
  66.8 9.2 %shard_map.274 = (f32[3,1024]{1,0:T(4,128)S(1)}, f32[3,1024]{1,0:T(4,128)S(1)}, f32[192,1024]{1,0:T(8,128)S(1)}) custom-call(s32[2]{0:T(128)S(1)} %add_convert_fusion.13.refs_0_, bf16[192,1024]{1,0:T(8,128)(2,1)S(1)} %fusion.30.refs_1_, bf16[384,1024]{1,0:T(8,128)(2,1)S(1)} %collective-permute-done.1.refs_2_.refs_3_.refs_5_.refs_6_, ...), custom_call_target="tpu_custom_call" | custom-call | flops 6442450944 | bytes 3145728 | tf_op jit(solution)/shard_map/pallas_call | solution.py:101
  76.2 18.7 %collective-permute-start.3 = (bf16[192,1024]{1,0:T(8,128)(2,1)S(1)}, bf16[192,1024]{1,0:T(8,128)(2,1)S(1)}, u32[]{:S(2)}, u32[]{:S(2)}) collective-permute-start(bf16[192,1024]{1,0:T(8,128)(2,1)S(1)} %slice.121), channel_id=1, source_target_pairs={{0,8},{8,16},{16,24},{24,28},{28,20},{20,12},{12,4},{4,0},{1,9},{9... | collective-permute-start | bytes 1179656 | tf_op jit(solution)/shard_map/ppermute | solution.py:26
  94.9 17.5 %shard_map.275 = (f32[3,1024]{1,0:T(4,128)S(1)}, f32[3,1024]{1,0:T(4,128)S(1)}, f32[192,1024]{1,0:T(8,128)S(1)}) custom-call(s32[2]{0:T(128)S(1)} %add_convert_fusion.12.refs_0_, bf16[192,1024]{1,0:T(8,128)(2,1)S(1)} %fusion.30.refs_1_, bf16[384,1024]{1,0:T(8,128)(2,1)S(1)} %collective-permute-done.2.refs_2_.refs_3_.refs_5_.refs_6_, ...), custom_call_target="tpu_custom_call" | custom-call | flops 6442450944 | bytes 3145728 | tf_op jit(solution)/shard_map/pallas_call | solution.py:101
  112.4 8.7 %shard_map.276 = (f32[3,1024]{1,0:T(4,128)S(1)}, f32[3,1024]{1,0:T(4,128)S(1)}, f32[192,1024]{1,0:T(8,128)S(1)}) custom-call(s32[1]{0:T(128)S(6)} %convert_element_type.153.refs_0_, bf16[192,1024]{1,0:T(8,128)(2,1)S(1)} %fusion.30.refs_1_, bf16[192,1024]{1,0:T(8,128)(2,1)S(1)} %collective-permute-done.3.refs_2_.refs_5_, ...), custom_call_target="tpu_custom_call" | custom-call | flops 3221225472 | bytes 3145728 | tf_op jit(solution)/shard_map/pallas_call | solution.py:101
  125.8 41.3 %all-reduce.8.cloned.1.call-done = bf16[1024,768]{1,0:T(8,128)(2,1)} async-done(((bf16[1024,768]{1,0:T(8,128)(2,1)}), bf16[1024,768]{1,0:T(8,128)(2,1)}) %all-reduce.8.cloned.1.call-update) | async-done | bytes 1572880 | tf_op jit(solution)/shard_map/psum | solution.py:215
  167.1 2.6 fusion.24
  174.0 4.3 convert_reduce_fusion.4
  179.5 2.6 convolution_convert_fusion
  182.6 5.3 convolution_convert_fusion.1
  188.0 3.0 convolution_convert_fusion.3
  191.0 34.1 %all-reduce.10.cloned.1.call-done = bf16[1024,768]{1,0:T(8,128)(2,1)} async-done(((bf16[1024,768]{1,0:T(8,128)(2,1)}), bf16[1024,768]{1,0:T(8,128)(2,1)}) %all-reduce.10.cloned.1.call-update) | async-done | bytes 1572880 | tf_op jit(solution)/shard_map/psum | solution.py:215
  225.1 4.4 convert_reduce_fusion.1
  229.6 3.0 fusion.21
  240.0 8.4 %shard_map.277 = (f32[192,1024]{1,0:T(8,128)S(1)}, f32[1024,384]{1,0:T(8,128)S(1)}) custom-call(s32[1]{0:T(128)S(6)} %convert_element_type.153.refs_0_, bf16[192,1024]{1,0:T(8,128)(2,1)S(1)} %copy-done.27, bf16[192,1024]{1,0:T(8,128)(2,1)S(1)} %get-tuple-element.121.refs_2_, f32[3,1024]{1,0:T(4,128)S(1)} %copy-done.2, f32[3,1024]{1,0:T(4,128)S(1)} %reduce_sum.168.refs_4_, ...), custom_call_target="tpu_custom_call" | custom-call | flops 8053063680 | bytes 4718592 | tf_op jit(solution)/shard_map/pallas_call | solution.py:184
  251.0 18.0 %shard_map.278 = (f32[192,1024]{1,0:T(8,128)S(1)}, f32[1024,384]{1,0:T(8,128)S(1)}, f32[1024,384]{1,0:T(8,128)}) custom-call(s32[2]{0:T(128)S(1)} %copy-done.25, bf16[192,1024]{1,0:T(8,128)(2,1)S(1)} %copy-done.27, bf16[192,1024]{1,0:T(8,128)(2,1)S(1)} %get-tuple-element.121.refs_2_, f32[3,1024]{1,0:T(4,128)S(1)} %copy-done.2, ...), custom_call_target="tpu_custom_call" | custom-call | flops 16106127360 | bytes 4718592 | tf_op jit(solution)/shard_map/pallas_call | solution.py:184
  273.9 10.0 %shard_map.279 = (f32[192,1024]{1,0:T(8,128)S(1)}, f32[1024,384]{1,0:T(8,128)S(1)}, f32[1024,384]{1,0:T(8,128)}) custom-call(s32[2]{0:T(128)S(1)} %copy-done.23, bf16[192,1024]{1,0:T(8,128)(2,1)S(1)} %copy-done.27, bf16[192,1024]{1,0:T(8,128)(2,1)S(1)} %get-tuple-element.121.refs_2_, f32[3,1024]{1,0:T(4,128)S(1)} %copy-done.2, ...), custom_call_target="tpu_custom_call" | custom-call | flops 16106127360 | bytes 4718592 | tf_op jit(solution)/shard_map/pallas_call | solution.py:184
  283.9 7.5 %collective-permute-done.9 = bf16[1024,384]{1,0:T(8,128)(2,1)S(1)} collective-permute-done((bf16[1024,384]{1,0:T(8,128)(2,1)S(1)}, bf16[1024,384]{1,0:T(8,128)(2,1)S(1)}, u32[]{:S(2)}, u32[]{:S(2)}) %collective-permute-start.9) | collective-permute-done | bytes 786464 | tf_op jit(solution)/shard_map/ppermute | solution.py:26
  295.6 10.0 %shard_map.280 = (f32[192,1024]{1,0:T(8,128)S(1)}, f32[1024,384]{1,0:T(8,128)S(1)}, f32[1024,384]{1,0:T(8,128)}) custom-call(s32[2]{0:T(128)S(1)} %copy-done.21, bf16[192,1024]{1,0:T(8,128)(2,1)S(1)} %copy-done.27, bf16[192,1024]{1,0:T(8,128)(2,1)S(1)} %get-tuple-element.121.refs_2_, f32[3,1024]{1,0:T(4,128)S(1)} %copy-done.2, ...), custom_call_target="tpu_custom_call" | custom-call | flops 16106127360 | bytes 4718592 | tf_op jit(solution)/shard_map/pallas_call | solution.py:184
  305.6 5.2 collective-permute-done.10
  312.4 3.6 collective-permute-start.11
  316.3 9.3 %shard_map.281 = (f32[192,1024]{1,0:T(8,128)S(1)}, f32[1024,384]{1,0:T(8,128)S(1)}) custom-call(s32[1]{0:T(128)S(6)} %convert_element_type.153.refs_0_, bf16[192,1024]{1,0:T(8,128)(2,1)S(1)} %copy-done.27, bf16[192,1024]{1,0:T(8,128)(2,1)S(1)} %get-tuple-element.121.refs_2_, f32[3,1024]{1,0:T(4,128)S(1)} %copy-done.3, f32[3,1024]{1,0:T(4,128)S(1)} %reduce_sum.168.refs_4_, ...), custom_call_target="tpu_custom_call" | custom-call | flops 8053063680 | bytes 4718592 | tf_op jit(solution)/shard_map/pallas_call | solution.py:184
  327.4 3.8 collective-permute-done.11
  336.3 3.9 convolution_convert_fusion.4
  346.1 58.3 %all-reduce.14.cloned.1.call-done = (bf16[1024,768]{1,0:T(8,128)(2,1)}, bf16[1024,768]{1,0:T(8,128)(2,1)}) async-done(((bf16[1024,768]{1,0:T(8,128)(2,1)}, bf16[1024,768]{1,0:T(8,128)(2,1)}), (bf16[1024,768]{1,0:T(8,128)(2,1)}, bf16[1024,768]{1,0:T(8,128)(2,1)})) %all-reduce.14.cloned.1.call-update) | async-done | bytes 3145744 | tf_op jit(solution)/shard_map/psum | solution.py:215
  404.5 2.6 convert_reduce_fusion
  409.3 5.7 %add_convert_fusion = (bf16[1024,768]{1,0:T(8,128)(2,1)}, bf16[1024,768]{1,0:T(8,128)(2,1)}, f32[768]{0:T(1024)S(1)}) fusion(bf16[1024,768]{1,0:T(8,128)(2,1)S(1)} %copy-done.33, bf16[1024,768]{1,0:T(8,128)(2,1)S(1)} %copy-done.42, bf16[1024,768]{1,0:T(8,128)(2,1)S(1)} %copy-done.49, f32[1024]{0:T(1024)S(1)} %negate_multiply_fusion, ...), kind=kLoop, calls=%fused_computation.41 | loop fusion | flops 22805760 | bytes 12631040 | tf_op jit(solution)/shard_map/convert_element_type | solution.py:399
  415.1 39.5 %psum.53 = f32[5760]{0:T(1024)S(1)} all-reduce(f32[5760]{0:T(1024)S(1)} %concatenate.29), channel_id=1, replica_groups=mesh['dp'=8,'tensor'=4] {'dp'}, use_global_device_ids=true, to_apply=%region_23.24 | all-reduce | flops 5760 | bytes 46080 | tf_op jit(solution)/shard_map/psum | solution.py:211
  455.9 93.1 %all-reduce.12.cloned.1.call-done = (bf16[768,768]{0,1:T(8,128)(2,1)}, bf16[1536,768]{1,0:T(8,128)(2,1)}) async-done(((bf16[768,768]{0,1:T(8,128)(2,1)}, bf16[1536,768]{1,0:T(8,128)(2,1)}), (bf16[768,768]{0,1:T(8,128)(2,1)}, bf16[1536,768]{1,0:T(8,128)(2,1)})) %all-reduce.12.cloned.1.call-update) | async-done | bytes 3538960 | tf_op jit(solution)/shard_map/psum | solution.py:211
  (310 shorter events, 71.6 us)
Async XLA Ops:
  7.2 166.8 %copy-start = (bf16[768,768]{1,0:T(8,128)(2,1)S(1)}, bf16[768,768]{1,0:T(8,128)(2,1)}, u32[]{:S(2)}) copy-start(bf16[768,768]{1,0:T(8,128)(2,1)} %param.29) | copy-start | bytes 3538948
  7.2 159.8 %all-reduce.8.cloned.1.call-start = ((), (), s32[]{:S(2)}) async-start(), calls=%async_computation | async-start | bytes 3145728 | tf_op jit(solution)/shard_map/psum | solution.py:215
  14.5 20.7 %collective-permute-start.4 = (bf16[384,1024]{1,0:T(8,128)(2,1)S(1)}, bf16[384,1024]{1,0:T(8,128)(2,1)S(1)}, u32[]{:S(2)}, u32[]{:S(2)}) collective-permute-start(bf16[384,1024]{1,0:T(8,128)(2,1)S(1)} %add_convert_fusion.9.refs_2_.refs_3_.refs_5_.refs_6_), channel_id=1, source_target_pairs={{0,4},{8,0},{16,8},{24,16},{28,24},{20,28},{12,20},{4,12},{1,5},{9... | collective-permute-start | bytes 2359304 | tf_op jit(solution)/shard_map/ppermute | solution.py:26
  17.4 19.8 %collective-permute-start = (bf16[384,1024]{1,0:T(8,128)(2,1)S(1)}, bf16[384,1024]{1,0:T(8,128)(2,1)S(1)}, u32[]{:S(2)}, u32[]{:S(2)}) collective-permute-start(bf16[384,1024]{1,0:T(8,128)(2,1)S(1)} %add_convert_fusion.9.refs_2_.refs_3_.refs_5_.refs_6_), channel_id=1, source_target_pairs={{0,8},{8,16},{16,24},{24,28},{28,20},{20,12},{12,4},{4,0},{1,9},{9... | collective-permute-start | bytes 2359304 | tf_op jit(solution)/shard_map/ppermute | solution.py:26
  35.2 19.0 %collective-permute-start.5 = (bf16[384,1024]{1,0:T(8,128)(2,1)S(1)}, bf16[384,1024]{1,0:T(8,128)(2,1)S(1)}, u32[]{:S(2)}, u32[]{:S(2)}) collective-permute-start(bf16[384,1024]{1,0:T(8,128)(2,1)S(1)} %collective-permute-done.4.refs_4_.refs_5_.refs_7_.refs_8_), channel_id=1, source_target_pairs={{0,4},{8,0},{16,8},{24,16},{28,24},{20,28},{12,20},{4,12},{1,5},{9... | collective-permute-start | bytes 2359304 | tf_op jit(solution)/shard_map/ppermute | solution.py:26
  37.2 18.7 %collective-permute-start.1 = (bf16[384,1024]{1,0:T(8,128)(2,1)S(1)}, bf16[384,1024]{1,0:T(8,128)(2,1)S(1)}, u32[]{:S(2)}, u32[]{:S(2)}) collective-permute-start(bf16[384,1024]{1,0:T(8,128)(2,1)S(1)} %collective-permute-done.refs_2_.refs_3_.refs_5_.refs_6_), channel_id=1, source_target_pairs={{0,8},{8,16},{16,24},{24,28},{28,20},{20,12},{12,4},{4,0},{1,9},{9... | collective-permute-start | bytes 2359304 | tf_op jit(solution)/shard_map/ppermute | solution.py:26
  37.5 57.4 %copy-start.24 = (s32[2]{0:T(128)}, s32[2]{0:T(128)S(1)}, u32[]{:S(2)}) copy-start(s32[2]{0:T(128)S(1)} %add_convert_fusion.12.refs_0_) | copy-start | bytes 28
  39.6 72.8 %copy-start.26 = (bf16[192,1024]{1,0:T(8,128)(2,1)}, bf16[192,1024]{1,0:T(8,128)(2,1)S(1)}, u32[]{:S(2)}) copy-start(bf16[192,1024]{1,0:T(8,128)(2,1)S(1)} %fusion.30.refs_1_) | copy-start | bytes 1179652
  54.3 21.8 %collective-permute-start.6 = (bf16[384,1024]{1,0:T(8,128)(2,1)S(1)}, bf16[384,1024]{1,0:T(8,128)(2,1)S(1)}, u32[]{:S(2)}, u32[]{:S(2)}) collective-permute-start(bf16[384,1024]{1,0:T(8,128)(2,1)S(1)} %collective-permute-done.5.refs_4_.refs_5_.refs_7_.refs_8_), channel_id=1, source_target_pairs={{0,4},{8,0},{16,8},{24,16},{28,24},{20,28},{12,20},{4,12},{1,5},{9... | collective-permute-start | bytes 2359304 | tf_op jit(solution)/shard_map/ppermute | solution.py:26
  55.9 20.2 %collective-permute-start.2 = (bf16[384,1024]{1,0:T(8,128)(2,1)S(1)}, bf16[384,1024]{1,0:T(8,128)(2,1)S(1)}, u32[]{:S(2)}, u32[]{:S(2)}) collective-permute-start(bf16[384,1024]{1,0:T(8,128)(2,1)S(1)} %collective-permute-done.1.refs_2_.refs_3_.refs_5_.refs_6_), channel_id=1, source_target_pairs={{0,8},{8,16},{16,24},{24,28},{28,20},{20,12},{12,4},{4,0},{1,9},{9... | collective-permute-start | bytes 2359304 | tf_op jit(solution)/shard_map/ppermute | solution.py:26
  76.1 36.3 %collective-permute-start.7 = (bf16[192,1024]{1,0:T(8,128)(2,1)S(1)}, bf16[192,1024]{1,0:T(8,128)(2,1)S(1)}, u32[]{:S(2)}, u32[]{:S(2)}) collective-permute-start(bf16[192,1024]{1,0:T(8,128)(2,1)S(1)} %slice.122), channel_id=1, source_target_pairs={{0,4},{8,0},{16,8},{24,16},{28,24},{20,28},{12,20},{4,12},{1,5},{9... | collective-permute-start | bytes 1179656 | tf_op jit(solution)/shard_map/ppermute | solution.py:26
  76.2 36.2 %collective-permute-start.3 = (bf16[192,1024]{1,0:T(8,128)(2,1)S(1)}, bf16[192,1024]{1,0:T(8,128)(2,1)S(1)}, u32[]{:S(2)}, u32[]{:S(2)}) collective-permute-start(bf16[192,1024]{1,0:T(8,128)(2,1)S(1)} %slice.121), channel_id=1, source_target_pairs={{0,8},{8,16},{16,24},{24,28},{28,20},{20,12},{12,4},{4,0},{1,9},{9... | collective-permute-start | bytes 1179656 | tf_op jit(solution)/shard_map/ppermute | solution.py:26
  124.4 100.7 %all-reduce.10.cloned.1.call-start = ((), (), s32[]{:S(2)}) async-start(), calls=%async_computation.1 | async-start | bytes 3145728 | tf_op jit(solution)/shard_map/psum | solution.py:215
  182.1 222.3 %all-reduce.14.cloned.1.call-start = ((), (), s32[]{:S(2)}) async-start(), calls=%async_computation.3 | async-start | bytes 6291456 | tf_op jit(solution)/shard_map/psum | solution.py:215
  187.9 37.2 %copy-start.65 = (f32[768]{0:T(1024)S(1)}, f32[768]{0:T(1024)}, u32[]{:S(2)}) copy-start(f32[768]{0:T(1024)} %param.24) | copy-start | bytes 9220
  188.0 37.2 %copy-start.69 = (f32[1024]{0:T(1024)S(1)}, f32[1024]{0:T(1024)}, u32[]{:S(2)}) copy-start(f32[1024]{0:T(1024)} %copy-done.67) | copy-start | bytes 12292
  191.0 38.6 %copy-start.90 = (f32[1024]{0:T(1024)S(1)}, f32[1024]{0:T(1024)}, u32[]{:S(2)}) copy-start(f32[1024]{0:T(1024)} %copy-done.89) | copy-start | bytes 12292
  191.0 38.6 %copy-start.79 = (f32[1024]{0:T(1024)S(1)}, f32[1024]{0:T(1024)}, u32[]{:S(2)}) copy-start(f32[1024]{0:T(1024)} %copy-done.77) | copy-start | bytes 12292
  248.8 22.6 %collective-permute-start.8 = (bf16[1024,192]{1,0:T(8,128)(2,1)S(1)}, bf16[1024,192]{1,0:T(8,128)(2,1)S(1)}, u32[]{:S(2)}, u32[]{:S(2)}) collective-permute-start(bf16[1024,192]{1,0:T(8,128)(2,1)S(1)} %get-tuple-element.99), channel_id=1, source_target_pairs={{0,8},{8,16},{16,24},{24,28},{28,20},{20,12},{12,4},{4,0},{1,9},{9... | collective-permute-start | bytes 1179656 | tf_op jit(solution)/shard_map/ppermute | solution.py:26
  250.3 20.3 %collective-permute-start.12 = (bf16[1024,192]{1,0:T(8,128)(2,1)S(1)}, bf16[1024,192]{1,0:T(8,128)(2,1)S(1)}, u32[]{:S(2)}, u32[]{:S(2)}) collective-permute-start(bf16[1024,192]{1,0:T(8,128)(2,1)S(1)} %get-tuple-element.100), channel_id=1, source_target_pairs={{0,4},{8,0},{16,8},{24,16},{28,24},{20,28},{12,20},{4,12},{1,5},{9... | collective-permute-start | bytes 1179656 | tf_op jit(solution)/shard_map/ppermute | solution.py:26
  271.3 22.6 %collective-permute-start.13 = (bf16[1024,384]{1,0:T(8,128)(2,1)S(1)}, bf16[1024,384]{1,0:T(8,128)(2,1)S(1)}, u32[]{:S(2)}, u32[]{:S(2)}) collective-permute-start(bf16[1024,384]{1,0:T(8,128)(2,1)S(1)} %pad_maximum_fusion.4), channel_id=1, source_target_pairs={{0,4},{8,0},{16,8},{24,16},{28,24},{20,28},{12,20},{4,12},{1,5},{9... | collective-permute-start | bytes 2359304 | tf_op jit(solution)/shard_map/ppermute | solution.py:26
  271.8 19.5 %collective-permute-start.9 = (bf16[1024,384]{1,0:T(8,128)(2,1)S(1)}, bf16[1024,384]{1,0:T(8,128)(2,1)S(1)}, u32[]{:S(2)}, u32[]{:S(2)}) collective-permute-start(bf16[1024,384]{1,0:T(8,128)(2,1)S(1)} %pad_maximum_fusion.3), channel_id=1, source_target_pairs={{0,8},{8,16},{16,24},{24,28},{28,20},{20,12},{12,4},{4,0},{1,9},{9... | collective-permute-start | bytes 2359304 | tf_op jit(solution)/shard_map/ppermute | solution.py:26
  293.1 17.7 %collective-permute-start.10 = (bf16[1024,384]{1,0:T(8,128)(2,1)S(1)}, bf16[1024,384]{1,0:T(8,128)(2,1)S(1)}, u32[]{:S(2)}, u32[]{:S(2)}) collective-permute-start(bf16[1024,384]{1,0:T(8,128)(2,1)S(1)} %add_convert_fusion.8), channel_id=1, source_target_pairs={{0,8},{8,16},{16,24},{24,28},{28,20},{20,12},{12,4},{4,0},{1,9},{9... | collective-permute-start | bytes 2359304 | tf_op jit(solution)/shard_map/ppermute | solution.py:26
  294.1 22.0 %collective-permute-start.14 = (bf16[1024,384]{1,0:T(8,128)(2,1)S(1)}, bf16[1024,384]{1,0:T(8,128)(2,1)S(1)}, u32[]{:S(2)}, u32[]{:S(2)}) collective-permute-start(bf16[1024,384]{1,0:T(8,128)(2,1)S(1)} %add_convert_fusion.6), channel_id=1, source_target_pairs={{0,4},{8,0},{16,8},{24,16},{28,24},{20,28},{12,20},{4,12},{1,5},{9... | collective-permute-start | bytes 2359304 | tf_op jit(solution)/shard_map/ppermute | solution.py:26
  312.4 18.7 %collective-permute-start.11 = (bf16[1024,384]{1,0:T(8,128)(2,1)S(1)}, bf16[1024,384]{1,0:T(8,128)(2,1)S(1)}, u32[]{:S(2)}, u32[]{:S(2)}) collective-permute-start(bf16[1024,384]{1,0:T(8,128)(2,1)S(1)} %add_convert_fusion.7), channel_id=1, source_target_pairs={{0,8},{8,16},{16,24},{24,28},{28,20},{20,12},{12,4},{4,0},{1,9},{9... | collective-permute-start | bytes 2359304 | tf_op jit(solution)/shard_map/ppermute | solution.py:26
  316.2 17.3 %collective-permute-start.15 = (bf16[1024,384]{1,0:T(8,128)(2,1)S(1)}, bf16[1024,384]{1,0:T(8,128)(2,1)S(1)}, u32[]{:S(2)}, u32[]{:S(2)}) collective-permute-start(bf16[1024,384]{1,0:T(8,128)(2,1)S(1)} %add_convert_fusion.5), channel_id=1, source_target_pairs={{0,4},{8,0},{16,8},{24,16},{28,24},{20,28},{12,20},{4,12},{1,5},{9... | collective-permute-start | bytes 2359304 | tf_op jit(solution)/shard_map/ppermute | solution.py:26
  336.0 213.0 %all-reduce.12.cloned.1.call-start = ((), (), s32[]{:S(2)}) async-start(), calls=%async_computation.2 | async-start | bytes 7077888 | tf_op jit(solution)/shard_map/psum | solution.py:211
  344.6 59.8 %copy-start.33 = (bf16[1024,768]{1,0:T(8,128)(2,1)S(1)}, bf16[1024,768]{1,0:T(8,128)(2,1)}, u32[]{:S(2)}) copy-start(bf16[1024,768]{1,0:T(8,128)(2,1)} %param.17) | copy-start | bytes 4718596
  344.6 59.8 %copy-start.62 = (f32[1024]{0:T(1024)S(1)}, f32[1024]{0:T(1024)}, u32[]{:S(2)}) copy-start(f32[1024]{0:T(1024)} %copy-done.61) | copy-start | bytes 12292
  344.6 59.8 %copy-start.72 = (f32[768]{0:T(1024)S(1)}, f32[768]{0:T(1024)}, u32[]{:S(2)}) copy-start(f32[768]{0:T(1024)} %param.19) | copy-start | bytes 9220
  345.7 61.5 %copy-start.88 = (f32[1024]{0:T(1024)S(1)}, f32[1024]{0:T(1024)}, u32[]{:S(2)}) copy-start(f32[1024]{0:T(1024)} %copy-done.87) | copy-start | bytes 12292
  345.7 61.5 %copy-start.74 = (f32[1024]{0:T(1024)S(1)}, f32[1024]{0:T(1024)}, u32[]{:S(2)}) copy-start(f32[1024]{0:T(1024)} %copy-done.73) | copy-start | bytes 12292
  (94 other events, 518.6 us)
Sparse Core Ops, SparseCore 0:
  124.5 42.4 all-reduce.7
  182.2 42.8 all-reduce.9
  336.1 68.2 all-reduce.13
  408.5 140.4 all-reduce.11

commit v2 on v1

--- a/solution.py
+++ b/solution.py
@@ -49,24 +49,34 @@
     first_query = pl.program_id(0) * tile
 
     def block(k_ref, v_ref):
-        for head in range(heads):
-            rows = slice(head * HEAD_DIM, (head + 1) * HEAD_DIM)
-            scores = tdot(k_ref[rows, :], q_ref[rows, :], 0, 0)
-            if diagonal:
-                key_place = lax.broadcasted_iota(jnp.int32, scores.shape, 0)
-                query_place = lax.broadcasted_iota(jnp.int32, scores.shape, 1) + first_query
-                scores = jnp.where(key_place <= query_place, scores, MASKED_SCORE)
-            old = max_ref[head : head + 1, :]
-            new = jnp.maximum(old, jnp.max(scores, axis=0, keepdims=True))
-            weights = jnp.exp(scores - new)
-            shrink = jnp.exp(old - new)
-            max_ref[head : head + 1, :] = new
-            sum_ref[head : head + 1, :] = sum_ref[head : head + 1, :] * shrink + jnp.sum(
-                weights, axis=0, keepdims=True
-            )
-            acc_ref[rows, :] = acc_ref[rows, :] * shrink + tdot(
-                v_ref[rows, :], weights.astype(jnp.bfloat16), 1, 0
-            )
+        spans = [slice(head * HEAD_DIM, (head + 1) * HEAD_DIM) for head in range(heads)]
+        scores = [tdot(k_ref[rows, :], q_ref[rows, :], 0, 0) for rows in spans]
+        if diagonal:
+            key_place = lax.broadcasted_iota(jnp.int32, scores[0].shape, 0)
+            query_place = lax.broadcasted_iota(jnp.int32, scores[0].shape, 1) + first_query
+            allowed = key_place <= query_place
+            scores = [jnp.where(allowed, part, MASKED_SCORE) for part in scores]
+        olds = [max_ref[head : head + 1, :] for head in range(heads)]
+        sums = [sum_ref[head : head + 1, :] for head in range(heads)]
+        accs = [acc_ref[rows, :] for rows in spans]
+        news = [
+            jnp.maximum(old, jnp.max(part, axis=0, keepdims=True))
+            for old, part in zip(olds, scores)
+        ]
+        weights = [jnp.exp(part - new) for part, new in zip(scores, news)]
+        shrinks = [jnp.exp(old - new) for old, new in zip(olds, news)]
+        sums = [
+            total * shrink + jnp.sum(part, axis=0, keepdims=True)
+            for total, shrink, part in zip(sums, shrinks, weights)
+        ]
+        accs = [
+            acc * shrink + tdot(v_ref[rows, :], part.astype(jnp.bfloat16), 1, 0)
+            for acc, shrink, rows, part in zip(accs, shrinks, spans, weights)
+        ]
+        for head, rows in enumerate(spans):
+            max_ref[head : head + 1, :] = news[head]
+            sum_ref[head : head + 1, :] = sums[head]
+            acc_ref[rows, :] = accs[head]
 
     for index in range(blocks):
         k_ref, v_ref = kv_refs[2 * index : 2 * index + 2]
@@ -211,8 +221,40 @@
     return lax.psum(value, "dp")
 
 
+def partner(value, axis, mask):
+    pairs = [(source, source ^ mask) for source in range(lax.axis_size(axis))]
+    return lax.ppermute(value, axis, pairs)
+
+
+def sum_tokens_small(value):
+    mask = 1
+    while mask < lax.axis_size("dp"):
+        value = value + partner(value, "dp", mask)
+        mask *= 2
+    return value
+
+
+def rounded(value):
+    return lax.optimization_barrier(value.astype(jnp.bfloat16))
+
+
 def sum_tensor(value):
-    return lax.psum(value.astype(jnp.bfloat16), "tensor").astype(jnp.float32)
+    value = rounded(value)
+    core = lax.axis_index("tensor") % 2
+    half = value.shape[0] // 2
+    kept = lax.dynamic_slice_in_dim(value, core * half, half, 0)
+    sent = lax.dynamic_slice_in_dim(value, (1 - core) * half, half, 0)
+    total = kept.astype(jnp.float32) + partner(sent, "tensor", 1).astype(jnp.float32)
+    mask = 2
+    while mask < lax.axis_size("tensor"):
+        low = rounded(total)
+        total = low.astype(jnp.float32) + partner(low, "tensor", mask).astype(jnp.float32)
+        mask *= 2
+    low = rounded(total)
+    other = partner(low, "tensor", 1)
+    lower = jnp.where(core == 0, low, other)
+    upper = jnp.where(core == 0, other, low)
+    return jnp.concatenate([lower, upper], axis=0).astype(jnp.float32)
 
 
 def local(
@@ -267,23 +309,24 @@
         + query_value_bias[0][:, None]
     ).astype(jnp.bfloat16)
     query_t = query_t * jnp.bfloat16(scale)
-    for hop in (2, 3):
-        ups.append(ring_shift(ups[-1], 1))
-        downs.append(ring_shift(downs[-1], -1))
-    far_keys = ring_shift(ups[-1][:local_width], 1)
-    far_values = ring_shift(downs[-1][local_width:], -1)
-
     def whole_pair(array):
         return ((array, 0), (array, 1))
 
     own_pair = [whole_pair(kv_t)]
-    hop_pairs = [None] + [[whole_pair(ups[hop]), whole_pair(downs[hop])] for hop in (1, 2, 3)]
-    far_pair = [((far_keys, 0), (far_values, 0))]
+    hop_pairs = [None]
     hop_flags = [None] + [flags_of(-hop, hop) for hop in (1, 2, 3)]
     far_flags = flags_of(4)
-
     carried = attend_forward(far_flags, query_t, own_pair, None)
     for hop in (1, 2, 3):
+        ups[hop], downs[hop], carried = lax.optimization_barrier((ups[hop], downs[hop], carried))
+        hop_pairs.append([whole_pair(ups[hop]), whole_pair(downs[hop])])
+        if hop < 3:
+            ups.append(ring_shift(ups[hop], 1))
+            downs.append(ring_shift(downs[hop], -1))
+        else:
+            far_keys = ring_shift(ups[hop][:local_width], 1)
+            far_values = ring_shift(downs[hop][local_width:], -1)
+            far_pair = [((far_keys, 0), (far_values, 0))]
         carried = attend_forward(hop_flags[hop], query_t, hop_pairs[hop], carried)
     run_max, run_sum, acc = attend_forward(far_flags, query_t, far_pair, carried)
     log_total = run_max + jnp.log(run_sum)
@@ -307,8 +350,9 @@
     pre_grad = gelu_pull(hidden_grad)[0].astype(jnp.bfloat16)
     two_part = jnp.einsum("tf,df->td", pre_grad, expand_weight, preferred_element_type=jnp.float32)
     normed_two_grad = sum_tensor(two_part)
-    feed_part = jnp.dot(hidden_low, shrink_weight, preferred_element_type=jnp.float32)
-    block_output = (resid + sum_tensor(feed_part) + shrink_bias).astype(jnp.bfloat16)
+    feed_part = jnp.dot(
+        hidden_low, shrink_weight, preferred_element_type=jnp.float32
+    ).astype(jnp.bfloat16)
     grad_out32 = output_grad.astype(jnp.float32)
     shrink_weight_grad = jnp.einsum(
         "tf,td->fd", hidden_low, output_grad, preferred_element_type=jnp.float32
@@ -316,9 +360,9 @@
     expand_weight_grad = jnp.einsum(
         "td,tf->df", normed_two, pre_grad, preferred_element_type=jnp.float32
     )
-    feed_grads = sum_tokens(
+    feed_low = sum_tokens(
         jnp.concatenate([shrink_weight_grad, expand_weight_grad], axis=0).astype(jnp.bfloat16)
-    ).astype(jnp.float32)
+    )
     shrink_bias_grad = jnp.sum(grad_out32, axis=0)
     expand_bias_grad = jnp.sum(pre_grad.astype(jnp.float32), axis=0)
     unused_norm, norm_two_pull = jax.vjp(layer_norm, resid, feed_norm_gain, feed_norm_bias)
@@ -340,10 +384,16 @@
 
     query_sum = jnp.zeros((local_width, tok_rows), jnp.float32)
     query_sum, far_term = back(far_flags, far_pair, query_sum, False)
+    query_sum, feed_part = lax.optimization_barrier((query_sum, feed_part))
+    block_output = (resid + sum_tensor(feed_part) + shrink_bias).astype(jnp.bfloat16)
     far_low = far_term.astype(jnp.bfloat16)
     moving_up = ring_shift(far_low[:, :local_width], 1)
     moving_down = ring_shift(far_low[:, local_width:], -1)
     for hop in (3, 2, 1):
+        if hop == 1:
+            query_sum, feed_low, block_output = lax.optimization_barrier(
+                (query_sum, feed_low, block_output)
+            )
         query_sum, down_term, up_term = back(hop_flags[hop], hop_pairs[hop], query_sum, False)
         if hop == 3:
             up_sum = jnp.concatenate(
@@ -383,11 +433,12 @@
     kv_weight_grad = jnp.einsum(
         "td,tf->df", normed_one, kv_low, preferred_element_type=jnp.float32
     )
-    attn_grads = sum_tokens(
-        jnp.concatenate(
-            [query_weight_grad, kv_weight_grad, output_weight_grad_t], axis=1
-        ).astype(jnp.bfloat16)
-    ).astype(jnp.float32)
+    attn_low = jnp.concatenate(
+        [query_weight_grad, kv_weight_grad, output_weight_grad_t], axis=1
+    ).astype(jnp.bfloat16)
+    attn_low, feed_low = lax.optimization_barrier((attn_low, feed_low))
+    attn_grads = sum_tokens(attn_low).astype(jnp.float32)
+    feed_grads = feed_low.astype(jnp.float32)
     input_weight_grad = jnp.stack(
         [attn_grads[:, j * local_width : (j + 1) * local_width] for j in range(3)]
     )
@@ -408,7 +459,7 @@
         query_bias_grad,
         value_bias_grad,
     ]
-    joined = sum_tokens(jnp.concatenate(vectors))
+    joined = sum_tokens_small(jnp.concatenate(vectors))
     summed = []
     first = 0
     for vector in vectors:

time: 568 us -> 483 us (0.85)
  blocking collectives: 39.5 us -> 0 us
  waiting for transfers between devices: 252 us -> 213 us
  Pallas kernels: 109 us -> 80 us
  other arithmetic: 43 us -> 53.8 us
  starting transfers between devices: 37.3 us -> 44.4 us
    psum x3 -> x0, waiting for transfers between devices: 134 us -> none  [sum_tensor(): return lax.psum(value.astype(jnp.bfloat16), 'tensor').astype(jnp.float32)]
    ppermute x0 -> x15, waiting for transfers between devices: none -> 65.5 us  [partner(): return lax.ppermute(value, axis, pairs)]
    psum x1 -> x0, blocking collectives: 39.5 us -> none  [sum_tokens(): return lax.psum(value, 'dp')]
    pallas_call x5, Pallas kernels: 53.1 us -> 30.9 us  [attend_forward(): pl.pallas_call(functools.partial(forward_kernel, heads, len(blocks), diag...]
    psum x1 -> x2, waiting for transfers between devices: 93.1 us -> 110 us  [sum_tokens(): return lax.psum(value, 'dp')]
    ppermute x16, waiting for transfers between devices: 24.9 us -> 37.9 us  [ring_shift(): return lax.ppermute(value, 'dp', pairs)]
    ppermute x0 -> x15, starting transfers between devices: none -> 10.7 us  [partner(): return lax.ppermute(value, axis, pairs)]
    pallas_call x5, Pallas kernels: 55.8 us -> 49.1 us  [attend_backward(): pl.pallas_call(functools.partial(backward_kernel, heads, len(blocks), dia...]
  transfers between devices with their start and end apart: 20 -> 33, of which waited for: 9 -> 20; matrix products, arithmetic and copies ran while one was open for 8% -> 14% of each run, Pallas kernels for 16% -> 16%
where the time goes in v2:
time: 483 us; the launch traced here: 473 us
  waiting for transfers between devices  213 us (44%)
  Pallas kernels  80 us (17%)
  other arithmetic  53.8 us (11%)
  starting transfers between devices  44.4 us (9%)
  between operations  31.7 us (7%)
  matrix products  27.5 us (6%)
  local copies, waits for them, and re-layouts  22.5 us (5%)
    psum x2, waiting for transfers between devices, sum_tokens(): return lax.psum(value, 'dp')  110 us
    ppermute x15, waiting for transfers between devices, partner(): return lax.ppermute(value, axis, pairs)  65.5 us
    pallas_call x5, Pallas kernels, attend_backward(): pl.pallas_call(functools.partial(backward_kernel, heads, len(blocks), dia...  49.1 us
    ppermute x16, waiting for transfers between devices, ring_shift(): return lax.ppermute(value, 'dp', pairs)  37.9 us
    ppermute x16, starting transfers between devices, ring_shift(): return lax.ppermute(value, 'dp', pairs)  33.6 us
    pallas_call x5, Pallas kernels, attend_forward(): pl.pallas_call(functools.partial(forward_kernel, heads, len(blocks), diag...  30.9 us
    ppermute x15, starting transfers between devices, partner(): return lax.ppermute(value, axis, pairs)  10.7 us
    reduce_sum x4, other arithmetic, layer_norm(): return centred * lax.rsqrt(spread + EPSILON) * gain + bias_vec  10.6 us
  transfers between devices with their start and end apart: 33, of which 20 were waited for; matrix products, arithmetic and copies ran while one was open for 14% of the time, Pallas kernels for 16%

profile of v2, /device:TPU:0, one launch (start us, length us, event | category | flops | bytes accessed | tf_op | source)
XLA Modules:
  0.0 473.4 jit_solution(10500439101588785756)
XLA Ops:
  14.5 2.9 collective-permute-start.1
  29.5 6.1 %shard_map.272 = (f32[3,1024]{1,0:T(4,128)S(1)}, f32[3,1024]{1,0:T(4,128)S(1)}, f32[192,1024]{1,0:T(8,128)S(1)}) custom-call(s32[1]{0:T(128)S(6)} %convert_element_type.228.refs_0_, bf16[192,1024]{1,0:T(8,128)(2,1)S(1)} %fusion.30.refs_1_, bf16[384,1024]{1,0:T(8,128)(2,1)S(1)} %add_convert_fusion.17.refs_2_.refs_3_.refs_5_.refs_6_, ...), custom_call_target="tpu_custom_call" | custom-call | flops 3221225472 | bytes 3145728 | tf_op jit(solution)/shard_map/pallas_call | solution.py:111
  50.0 11.4 %shard_map.273 = (f32[3,1024]{1,0:T(4,128)S(1)}, f32[3,1024]{1,0:T(4,128)S(1)}, f32[192,1024]{1,0:T(8,128)S(1)}) custom-call(s32[2]{0:T(128)S(1)} %add_convert_fusion.21.refs_0_, bf16[192,1024]{1,0:T(8,128)(2,1)S(1)} %copy-done.24, bf16[384,1024]{1,0:T(8,128)(2,1)S(1)} %collective-permute-done.refs_2_.refs_3_.refs_5_.refs_6_, ...), custom_call_target="tpu_custom_call" | custom-call | flops 6442450944 | bytes 3145728 | tf_op jit(solution)/shard_map/pallas_call | solution.py:111
  63.7 6.8 %shard_map.274 = (f32[3,1024]{1,0:T(4,128)S(1)}, f32[3,1024]{1,0:T(4,128)S(1)}, f32[192,1024]{1,0:T(8,128)S(1)}) custom-call(s32[2]{0:T(128)S(1)} %add_convert_fusion.20.refs_0_, bf16[192,1024]{1,0:T(8,128)(2,1)S(1)} %copy-done.24, bf16[384,1024]{1,0:T(8,128)(2,1)S(1)} %collective-permute-done.2.refs_2_.refs_3_.refs_5_.refs_6_, ...), custom_call_target="tpu_custom_call" | custom-call | flops 6442450944 | bytes 3145728 | tf_op jit(solution)/shard_map/pallas_call | solution.py:111
  70.5 9.5 %collective-permute-done.4.refs_2_.refs_3_.refs_5_.refs_6_ = bf16[384,1024]{1,0:T(8,128)(2,1)S(1)} collective-permute-done((bf16[384,1024]{1,0:T(8,128)(2,1)S(1)}, bf16[384,1024]{1,0:T(8,128)(2,1)S(1)}, u32[]{:S(2)}, u32[]{:S(2)}) %collective-permute-start.4) | collective-permute-done | bytes 786464 | tf_op jit(solution)/shard_map/ppermute | solution.py:26
  84.3 5.9 %collective-permute-done.7.refs_3_.refs_6_ = bf16[192,1024]{1,0:T(8,128)(2,1)S(1)} collective-permute-done((bf16[192,1024]{1,0:T(8,128)(2,1)S(1)}, bf16[192,1024]{1,0:T(8,128)(2,1)S(1)}, u32[]{:S(2)}, u32[]{:S(2)}) %collective-permute-start.7) | collective-permute-done | bytes 393248 | tf_op jit(solution)/shard_map/ppermute | solution.py:26
  90.8 5.7 %shard_map.276 = (f32[3,1024]{1,0:T(4,128)S(1)}, f32[3,1024]{1,0:T(4,128)S(1)}, f32[192,1024]{1,0:T(8,128)S(1)}) custom-call(s32[1]{0:T(128)S(6)} %convert_element_type.228.refs_0_, bf16[192,1024]{1,0:T(8,128)(2,1)S(1)} %copy-done.25, bf16[192,1024]{1,0:T(8,128)(2,1)S(1)} %collective-permute-done.6.refs_2_.refs_5_, ...), custom_call_target="tpu_custom_call" | custom-call | flops 3221225472 | bytes 3145728 | tf_op jit(solution)/shard_map/pallas_call | solution.py:111
  101.7 2.6 collective-permute-done.8
  107.4 18.2 %collective-permute-done.9 = bf16[512,768]{1,0:T(8,128)(2,1)S(1)} collective-permute-done((bf16[512,768]{1,0:T(8,128)(2,1)S(1)}, bf16[512,768]{1,0:T(8,128)(2,1)S(1)}, u32[]{:S(2)}, u32[]{:S(2)}) %collective-permute-start.9) | collective-permute-done | bytes 786464 | tf_op jit(solution)/shard_map/ppermute | solution.py:226
  134.9 4.3 convert_reduce_fusion.4
  148.8 14.1 %collective-permute-done.12 = bf16[512,768]{1,0:T(8,128)(2,1)S(1)} collective-permute-done((bf16[512,768]{1,0:T(8,128)(2,1)S(1)}, bf16[512,768]{1,0:T(8,128)(2,1)S(1)}, u32[]{:S(2)}, u32[]{:S(2)}) %collective-permute-start.12) | collective-permute-done | bytes 786464 | tf_op jit(solution)/shard_map/ppermute | solution.py:226
  165.7 5.1 %convolution_convert_fusion = bf16[1024,768]{1,0:T(8,128)(2,1)} fusion(bf16[768,768]{1,0:T(8,128)(2,1)S(1)} %copy-done, f32[1024,768]{1,0:T(8,128)} %copy-done.104, f32[768]{0:T(1024)} %param.28), kind=kOutput, calls=%fused_computation.53 | convolution fusion | flops 1216610304 | bytes 5901312 | tf_op jit(solution)/shard_map/dot_general | solution.py:353
  173.1 3.0 fusion.10
  176.2 4.0 fusion.21
  180.2 3.5 convert_reduce_fusion.5
  188.6 8.4 %shard_map.277 = (f32[192,1024]{1,0:T(8,128)S(1)}, f32[1024,384]{1,0:T(8,128)S(1)}) custom-call(s32[1]{0:T(128)S(6)} %convert_element_type.228.refs_0_, bf16[192,1024]{1,0:T(8,128)(2,1)S(1)} %copy-done.26, bf16[192,1024]{1,0:T(8,128)(2,1)S(1)} %get-tuple-element.166.refs_2_, f32[3,1024]{1,0:T(4,128)S(1)} %copy-done.2, f32[3,1024]{1,0:T(4,128)S(1)} %reduce_sum.168.refs_4_, ...), custom_call_target="tpu_custom_call" | custom-call | flops 8053063680 | bytes 4718592 | tf_op jit(solution)/shard_map/pallas_call | solution.py:194
  199.6 2.7 shard_map.278
  205.5 8.2 %collective-permute-done.21 = bf16[1024,192]{1,0:T(8,128)(2,1)S(1)} collective-permute-done((bf16[1024,192]{1,0:T(8,128)(2,1)S(1)}, bf16[1024,192]{1,0:T(8,128)(2,1)S(1)}, u32[]{:S(2)}, u32[]{:S(2)}) %collective-permute-start.21) | collective-permute-done | bytes 393248 | tf_op jit(solution)/shard_map/ppermute | solution.py:26
  215.7 5.6 %collective-permute-start.18 = (bf16[1024,384]{1,0:T(8,128)(2,1)S(1)}, bf16[1024,384]{1,0:T(8,128)(2,1)S(1)}, u32[]{:S(2)}, u32[]{:S(2)}) collective-permute-start(bf16[1024,384]{1,0:T(8,128)(2,1)S(1)} %pad_maximum_fusion.6), channel_id=1, source_target_pairs={{0,8},{8,16},{16,24},{24,28},{28,20},{20,12},{12,4},{4,0},{1,9},{9... | collective-permute-start | bytes 2359304 | tf_op jit(solution)/shard_map/ppermute | solution.py:26
  221.3 2.7 collective-permute-done.15
  224.4 10.4 %shard_map.279 = (f32[192,1024]{1,0:T(8,128)S(1)}, f32[1024,384]{1,0:T(8,128)S(1)}, f32[1024,384]{1,0:T(8,128)}) custom-call(s32[2]{0:T(128)S(1)} %copy-done.20, bf16[192,1024]{1,0:T(8,128)(2,1)S(1)} %copy-done.26, bf16[192,1024]{1,0:T(8,128)(2,1)S(1)} %get-tuple-element.166.refs_2_, f32[3,1024]{1,0:T(4,128)S(1)} %copy-done.2, ...), custom_call_target="tpu_custom_call" | custom-call | flops 16106127360 | bytes 4718592 | tf_op jit(solution)/shard_map/pallas_call | solution.py:194
  234.8 7.2 %collective-permute-done.18 = bf16[1024,384]{1,0:T(8,128)(2,1)S(1)} collective-permute-done((bf16[1024,384]{1,0:T(8,128)(2,1)S(1)}, bf16[1024,384]{1,0:T(8,128)(2,1)S(1)}, u32[]{:S(2)}, u32[]{:S(2)}) %collective-permute-start.18) | collective-permute-done | bytes 786464 | tf_op jit(solution)/shard_map/ppermute | solution.py:26
  248.1 10.2 %collective-permute-start.23 = (bf16[1024,384]{1,0:T(8,128)(2,1)}, bf16[1024,384]{1,0:T(8,128)(2,1)}, u32[]{:S(2)}, u32[]{:S(2)}) collective-permute-start(bf16[1024,384]{1,0:T(8,128)(2,1)} %add_convert_fusion.8), channel_id=1, source_target_pairs={{0,4},{8,0},{16,8},{24,16},{28,24},{20,28},{12,20},{4,12},{1,5},{9... | collective-permute-start | bytes 2359304 | tf_op jit(solution)/shard_map/ppermute | solution.py:26
  260.5 44.3 %all-reduce.4.cloned.1.call-done = bf16[1536,768]{1,0:T(8,128)(2,1)} async-done(((bf16[1536,768]{1,0:T(8,128)(2,1)}), bf16[1536,768]{1,0:T(8,128)(2,1)}) %all-reduce.4.cloned.1.call-update) | async-done | bytes 2359312 | tf_op jit(solution)/shard_map/psum | solution.py:221
  304.7 18.1 %shard_map.280 = (f32[192,1024]{1,0:T(8,128)S(1)}, f32[1024,384]{1,0:T(8,128)S(1)}, f32[1024,384]{1,0:T(8,128)}) custom-call(s32[2]{0:T(128)S(1)} %copy-done.18, bf16[192,1024]{1,0:T(8,128)(2,1)S(1)} %copy-done.27, bf16[192,1024]{1,0:T(8,128)(2,1)S(1)} %get-tuple-element.166.refs_2_, f32[3,1024]{1,0:T(4,128)S(1)} %copy-done.2, ...), custom_call_target="tpu_custom_call" | custom-call | flops 16106127360 | bytes 4718592 | tf_op jit(solution)/shard_map/pallas_call | solution.py:194
  328.1 9.5 %shard_map.281 = (f32[192,1024]{1,0:T(8,128)S(1)}, f32[1024,384]{1,0:T(8,128)S(1)}) custom-call(s32[1]{0:T(128)S(6)} %convert_element_type.228.refs_0_, bf16[192,1024]{1,0:T(8,128)(2,1)S(1)} %copy-done.27, bf16[192,1024]{1,0:T(8,128)(2,1)S(1)} %get-tuple-element.166.refs_2_, f32[3,1024]{1,0:T(4,128)S(1)} %copy-done.2, f32[3,1024]{1,0:T(4,128)S(1)} %reduce_sum.168.refs_4_, ...), custom_call_target="tpu_custom_call" | custom-call | flops 8053063680 | bytes 4718592 | tf_op jit(solution)/shard_map/pallas_call | solution.py:194
  339.3 4.9 %collective-permute-done.20 = bf16[1024,384]{1,0:T(8,128)(2,1)S(1)} collective-permute-done((bf16[1024,384]{1,0:T(8,128)(2,1)S(1)}, bf16[1024,384]{1,0:T(8,128)(2,1)S(1)}, u32[]{:S(2)}, u32[]{:S(2)}) %collective-permute-start.20) | collective-permute-done | bytes 786464 | tf_op jit(solution)/shard_map/ppermute | solution.py:26
  351.7 17.6 %collective-permute-done.26 = bf16[512,768]{1,0:T(8,128)(2,1)S(1)} collective-permute-done((bf16[512,768]{1,0:T(8,128)(2,1)S(1)}, bf16[512,768]{1,0:T(8,128)(2,1)S(1)}, u32[]{:S(2)}, u32[]{:S(2)}) %collective-permute-start.26) | collective-permute-done | bytes 786464 | tf_op jit(solution)/shard_map/ppermute | solution.py:226
  374.8 2.7 fusion.22
  377.7 5.3 %convert_reduce_fusion.3 = (f32[768]{0:T(1024)S(1)}, bf16[1024,768]{1,0:T(8,128)(2,1)}) fusion(bf16[1024,768]{1,0:T(8,128)(2,1)S(1)} %copy-done.54, f32[1024]{0:T(1024)S(1)} %negate_multiply_fusion, f32[1024]{0:T(1024)S(1)} %multiply_multiply_fusion.2, f32[1024]{0:T(1024)S(1)} %copy-done.72, f32[1024]{0:T(1024)S(1)} %copy-done.84, f32[768]{0:T(1024)S(1)} %copy-done.80, ...), kind=kLoop, calls=%fused_computation.18 | loop fusion | flops 26737920 | bytes 9482240 | tf_op jit(solution)/shard_map/reduce_sum | solution.py:366
  384.8 4.2 fusion.47
  389.0 65.7 %all-reduce.6.cloned.1.call-done = bf16[768,768]{0,1:T(8,128)(2,1)} async-done(((bf16[768,768]{0,1:T(8,128)(2,1)}), bf16[768,768]{0,1:T(8,128)(2,1)}) %all-reduce.6.cloned.1.call-update) | async-done | bytes 1179664 | tf_op jit(solution)/shard_map/psum | solution.py:221
  (351 shorter events, 110.7 us)
Async XLA Ops:
  7.2 297.5 %all-reduce.4.cloned.1.call-start = ((), (), s32[]{:S(2)}) async-start(), calls=%async_computation | async-start | bytes 4718592 | tf_op jit(solution)/shard_map/psum | solution.py:221
  14.5 22.7 %collective-permute-start.1 = (bf16[384,1024]{1,0:T(8,128)(2,1)S(1)}, bf16[384,1024]{1,0:T(8,128)(2,1)S(1)}, u32[]{:S(2)}, u32[]{:S(2)}) collective-permute-start(bf16[384,1024]{1,0:T(8,128)(2,1)S(1)} %add_convert_fusion.17.refs_2_.refs_3_.refs_5_.refs_6_), channel_id=1, source_target_pairs={{0,4},{8,0},{16,8},{24,16},{28,24},{20,28},{12,20},{4,12},{1,5},{9... | collective-permute-start | bytes 2359304 | tf_op jit(solution)/shard_map/ppermute | solution.py:26
  17.4 19.7 %collective-permute-start = (bf16[384,1024]{1,0:T(8,128)(2,1)S(1)}, bf16[384,1024]{1,0:T(8,128)(2,1)S(1)}, u32[]{:S(2)}, u32[]{:S(2)}) collective-permute-start(bf16[384,1024]{1,0:T(8,128)(2,1)S(1)} %add_convert_fusion.17.refs_2_.refs_3_.refs_5_.refs_6_), channel_id=1, source_target_pairs={{0,8},{8,16},{16,24},{24,28},{28,20},{20,12},{12,4},{4,0},{1,9},{9... | collective-permute-start | bytes 2359304 | tf_op jit(solution)/shard_map/ppermute | solution.py:26
  37.2 24.3 %collective-permute-start.2 = (bf16[384,1024]{1,0:T(8,128)(2,1)S(1)}, bf16[384,1024]{1,0:T(8,128)(2,1)S(1)}, u32[]{:S(2)}, u32[]{:S(2)}) collective-permute-start(bf16[384,1024]{1,0:T(8,128)(2,1)S(1)} %collective-permute-done.refs_2_.refs_3_.refs_5_.refs_6_), channel_id=1, source_target_pairs={{0,8},{8,16},{16,24},{24,28},{28,20},{20,12},{12,4},{4,0},{1,9},{9... | collective-permute-start | bytes 2359304 | tf_op jit(solution)/shard_map/ppermute | solution.py:26
  39.3 22.2 %collective-permute-start.3 = (bf16[384,1024]{1,0:T(8,128)(2,1)S(1)}, bf16[384,1024]{1,0:T(8,128)(2,1)}, u32[]{:S(2)}, u32[]{:S(2)}) collective-permute-start(bf16[384,1024]{1,0:T(8,128)(2,1)S(1)} %collective-permute-done.1.refs_4_.refs_5_.refs_7_.refs_8_), channel_id=1, source_target_pairs={{0,4},{8,0},{16,8},{24,16},{28,24},{20,28},{12,20},{4,12},{1,5},{9... | collective-permute-start | bytes 2359304 | tf_op jit(solution)/shard_map/ppermute | solution.py:26
  61.5 18.5 %collective-permute-start.4 = (bf16[384,1024]{1,0:T(8,128)(2,1)S(1)}, bf16[384,1024]{1,0:T(8,128)(2,1)S(1)}, u32[]{:S(2)}, u32[]{:S(2)}) collective-permute-start(bf16[384,1024]{1,0:T(8,128)(2,1)S(1)} %collective-permute-done.2.refs_2_.refs_3_.refs_5_.refs_6_), channel_id=1, source_target_pairs={{0,8},{8,16},{16,24},{24,28},{28,20},{20,12},{12,4},{4,0},{1,9},{9... | collective-permute-start | bytes 2359304 | tf_op jit(solution)/shard_map/ppermute | solution.py:26
  61.5 18.7 %collective-permute-start.5 = (bf16[384,1024]{1,0:T(8,128)(2,1)}, bf16[384,1024]{1,0:T(8,128)(2,1)S(1)}, u32[]{:S(2)}, u32[]{:S(2)}) collective-permute-start(bf16[384,1024]{1,0:T(8,128)(2,1)} %collective-permute-done.3.refs_4_.refs_5_.refs_7_.refs_8_), channel_id=1, source_target_pairs={{0,4},{8,0},{16,8},{24,16},{28,24},{20,28},{12,20},{4,12},{1,5},{9... | collective-permute-start | bytes 2359304 | tf_op jit(solution)/shard_map/ppermute | solution.py:26
  80.3 10.0 %collective-permute-start.7 = (bf16[192,1024]{1,0:T(8,128)(2,1)S(1)}, bf16[192,1024]{1,0:T(8,128)(2,1)S(1)}, u32[]{:S(2)}, u32[]{:S(2)}) collective-permute-start(bf16[192,1024]{1,0:T(8,128)(2,1)S(1)} %slice.96), channel_id=1, source_target_pairs={{0,4},{8,0},{16,8},{24,16},{28,24},{20,28},{12,20},{4,12},{1,5},{9... | collective-permute-start | bytes 1179656 | tf_op jit(solution)/shard_map/ppermute | solution.py:26
  82.0 8.7 %collective-permute-start.6 = (bf16[192,1024]{1,0:T(8,128)(2,1)S(1)}, bf16[192,1024]{1,0:T(8,128)(2,1)S(1)}, u32[]{:S(2)}, u32[]{:S(2)}) collective-permute-start(bf16[192,1024]{1,0:T(8,128)(2,1)S(1)} %slice.95), channel_id=1, source_target_pairs={{0,8},{8,16},{16,24},{24,28},{28,20},{20,12},{12,4},{4,0},{1,9},{9... | collective-permute-start | bytes 1179656 | tf_op jit(solution)/shard_map/ppermute | solution.py:26
  101.7 2.6 collective-permute-start.8
  105.9 19.6 %collective-permute-start.9 = (bf16[512,768]{1,0:T(8,128)(2,1)S(1)}, bf16[512,768]{1,0:T(8,128)(2,1)S(1)}, u32[]{:S(2)}, u32[]{:S(2)}) collective-permute-start(bf16[512,768]{1,0:T(8,128)(2,1)S(1)} %add_convert_fusion.16), channel_id=1, source_target_pairs={{0,2},{1,3},{2,0},{3,1},{4,6},{5,7},{6,4},{7,5},{8,10},{9,11},{10,... | collective-permute-start | bytes 2359304 | tf_op jit(solution)/shard_map/ppermute | solution.py:226
  126.6 2.6 collective-permute-start.10
  140.8 2.4 collective-permute-start.11
  143.3 19.7 %collective-permute-start.12 = (bf16[512,768]{1,0:T(8,128)(2,1)S(1)}, bf16[512,768]{1,0:T(8,128)(2,1)S(1)}, u32[]{:S(2)}, u32[]{:S(2)}) collective-permute-start(bf16[512,768]{1,0:T(8,128)(2,1)S(1)} %add_convert_fusion.14), channel_id=1, source_target_pairs={{0,2},{1,3},{2,0},{3,1},{4,6},{5,7},{6,4},{7,5},{8,10},{9,11},{10,... | collective-permute-start | bytes 2359304 | tf_op jit(solution)/shard_map/ppermute | solution.py:226
  164.0 6.8 %collective-permute-start.13 = (bf16[512,768]{1,0:T(8,128)(2,1)}, bf16[512,768]{1,0:T(8,128)(2,1)}, u32[]{:S(2)}, u32[]{:S(2)}) collective-permute-start(bf16[512,768]{1,0:T(8,128)(2,1)} %add_convert_fusion.13), channel_id=1, source_target_pairs={{0,1},{1,0},{2,3},{3,2},{4,5},{5,4},{6,7},{7,6},{8,9},{9,8},{10,11... | collective-permute-start | bytes 2359304 | tf_op jit(solution)/shard_map/ppermute | solution.py:226
  165.6 289.1 %all-reduce.6.cloned.1.call-start = ((), (), s32[]{:S(2)}) async-start(), calls=%async_computation.1 | async-start | bytes 2359296 | tf_op jit(solution)/shard_map/psum | solution.py:221
  197.5 17.7 %collective-permute-start.17 = (bf16[1024,192]{1,0:T(8,128)(2,1)S(1)}, bf16[1024,192]{1,0:T(8,128)(2,1)S(1)}, u32[]{:S(2)}, u32[]{:S(2)}) collective-permute-start(bf16[1024,192]{1,0:T(8,128)(2,1)S(1)} %get-tuple-element.144), channel_id=1, source_target_pairs={{0,8},{8,16},{16,24},{24,28},{28,20},{20,12},{12,4},{4,0},{1,9},{9... | collective-permute-start | bytes 1179656 | tf_op jit(solution)/shard_map/ppermute | solution.py:26
  197.6 16.2 %collective-permute-start.21 = (bf16[1024,192]{1,0:T(8,128)(2,1)S(1)}, bf16[1024,192]{1,0:T(8,128)(2,1)S(1)}, u32[]{:S(2)}, u32[]{:S(2)}) collective-permute-start(bf16[1024,192]{1,0:T(8,128)(2,1)S(1)} %get-tuple-element.145), channel_id=1, source_target_pairs={{0,4},{8,0},{16,8},{24,16},{28,24},{20,28},{12,20},{4,12},{1,5},{9... | collective-permute-start | bytes 1179656 | tf_op jit(solution)/shard_map/ppermute | solution.py:26
  199.6 4.3 collective-permute-start.14
  204.0 20.0 %collective-permute-start.15 = (bf16[512,768]{1,0:T(8,128)(2,1)S(1)}, bf16[512,768]{1,0:T(8,128)(2,1)S(1)}, u32[]{:S(2)}, u32[]{:S(2)}) collective-permute-start(bf16[512,768]{1,0:T(8,128)(2,1)S(1)} %add_convert_fusion.12), channel_id=1, source_target_pairs={{0,2},{1,3},{2,0},{3,1},{4,6},{5,7},{6,4},{7,5},{8,10},{9,11},{10,... | collective-permute-start | bytes 2359304 | tf_op jit(solution)/shard_map/ppermute | solution.py:226
  214.4 32.6 %collective-permute-start.22 = (bf16[1024,384]{1,0:T(8,128)(2,1)S(1)}, bf16[1024,384]{1,0:T(8,128)(2,1)S(1)}, u32[]{:S(2)}, u32[]{:S(2)}) collective-permute-start(bf16[1024,384]{1,0:T(8,128)(2,1)S(1)} %pad_maximum_fusion.7), channel_id=1, source_target_pairs={{0,4},{8,0},{16,8},{24,16},{28,24},{20,28},{12,20},{4,12},{1,5},{9... | collective-permute-start | bytes 2359304 | tf_op jit(solution)/shard_map/ppermute | solution.py:26
  215.7 26.3 %collective-permute-start.18 = (bf16[1024,384]{1,0:T(8,128)(2,1)S(1)}, bf16[1024,384]{1,0:T(8,128)(2,1)S(1)}, u32[]{:S(2)}, u32[]{:S(2)}) collective-permute-start(bf16[1024,384]{1,0:T(8,128)(2,1)S(1)} %pad_maximum_fusion.6), channel_id=1, source_target_pairs={{0,8},{8,16},{16,24},{24,28},{28,20},{20,12},{12,4},{4,0},{1,9},{9... | collective-permute-start | bytes 2359304 | tf_op jit(solution)/shard_map/ppermute | solution.py:26
  224.3 34.0 %collective-permute-start.16 = (bf16[512,768]{1,0:T(8,128)(2,1)S(1)}, bf16[512,768]{1,0:T(8,128)(2,1)S(1)}, u32[]{:S(2)}, u32[]{:S(2)}) collective-permute-start(bf16[512,768]{1,0:T(8,128)(2,1)S(1)} %add_convert_fusion.11), channel_id=1, source_target_pairs={{0,1},{1,0},{2,3},{3,2},{4,5},{5,4},{6,7},{7,6},{8,9},{9,8},{10,11... | collective-permute-start | bytes 2359304 | tf_op jit(solution)/shard_map/ppermute | solution.py:226
  244.5 78.3 %collective-permute-start.19 = (bf16[1024,384]{1,0:T(8,128)(2,1)}, bf16[1024,384]{1,0:T(8,128)(2,1)}, u32[]{:S(2)}, u32[]{:S(2)}) collective-permute-start(bf16[1024,384]{1,0:T(8,128)(2,1)} %add_convert_fusion.10), channel_id=1, source_target_pairs={{0,8},{8,16},{16,24},{24,28},{28,20},{20,12},{12,4},{4,0},{1,9},{9... | collective-permute-start | bytes 2359304 | tf_op jit(solution)/shard_map/ppermute | solution.py:26
  248.1 76.6 %collective-permute-start.23 = (bf16[1024,384]{1,0:T(8,128)(2,1)}, bf16[1024,384]{1,0:T(8,128)(2,1)}, u32[]{:S(2)}, u32[]{:S(2)}) collective-permute-start(bf16[1024,384]{1,0:T(8,128)(2,1)} %add_convert_fusion.8), channel_id=1, source_target_pairs={{0,4},{8,0},{16,8},{24,16},{28,24},{20,28},{12,20},{4,12},{1,5},{9... | collective-permute-start | bytes 2359304 | tf_op jit(solution)/shard_map/ppermute | solution.py:26
  324.7 19.6 %collective-permute-start.20 = (bf16[1024,384]{1,0:T(8,128)(2,1)S(1)}, bf16[1024,384]{1,0:T(8,128)(2,1)S(1)}, u32[]{:S(2)}, u32[]{:S(2)}) collective-permute-start(bf16[1024,384]{1,0:T(8,128)(2,1)S(1)} %add_convert_fusion.9), channel_id=1, source_target_pairs={{0,8},{8,16},{16,24},{24,28},{28,20},{20,12},{12,4},{4,0},{1,9},{9... | collective-permute-start | bytes 2359304 | tf_op jit(solution)/shard_map/ppermute | solution.py:26
  326.1 19.6 %collective-permute-start.24 = (bf16[1024,384]{1,0:T(8,128)(2,1)S(1)}, bf16[1024,384]{1,0:T(8,128)(2,1)S(1)}, u32[]{:S(2)}, u32[]{:S(2)}) collective-permute-start(bf16[1024,384]{1,0:T(8,128)(2,1)S(1)} %add_convert_fusion.7), channel_id=1, source_target_pairs={{0,4},{8,0},{16,8},{24,16},{28,24},{20,28},{12,20},{4,12},{1,5},{9... | collective-permute-start | bytes 2359304 | tf_op jit(solution)/shard_map/ppermute | solution.py:26
  349.6 19.6 %collective-permute-start.26 = (bf16[512,768]{1,0:T(8,128)(2,1)S(1)}, bf16[512,768]{1,0:T(8,128)(2,1)S(1)}, u32[]{:S(2)}, u32[]{:S(2)}) collective-permute-start(bf16[512,768]{1,0:T(8,128)(2,1)S(1)} %add_convert_fusion.5), channel_id=1, source_target_pairs={{0,2},{1,3},{2,0},{3,1},{4,6},{5,7},{6,4},{7,5},{8,10},{9,11},{10,... | collective-permute-start | bytes 2359304 | tf_op jit(solution)/shard_map/ppermute | solution.py:226
  369.5 3.0 collective-permute-start.27
  383.1 73.1 %collective-permute-start.28 = (f32[5760]{0:T(1024)S(1)}, f32[5760]{0:T(1024)S(1)}, u32[]{:S(2)}, u32[]{:S(2)}) collective-permute-start(f32[5760]{0:T(1024)S(1)} %concatenate.46), channel_id=1, source_target_pairs={{0,4},{4,0},{8,12},{12,8},{16,20},{20,16},{24,28},{28,24},{1,5},{5... | collective-permute-start | bytes 69128 | tf_op jit(solution)/shard_map/ppermute | solution.py:226
  456.2 3.9 collective-permute-start.29
  460.1 4.7 collective-permute-start.30
  (106 other events, 915.2 us)
Sparse Core Ops, SparseCore 0:
  165.7 138.9 all-reduce.3
  372.3 82.3 all-reduce.5
